TPU v7x, 32 devices: a whole 2x2x4 slice. The times are simulated.
32 devices in a mesh: pipe: 4 (over y, x), seq: 8 (over z, core).
Axes of the slice: x: 2, y: 2, z: 4, core: 2. Of those that a mesh axis runs over, the one named last changes fastest.
Arguments:
- queries: bfloat16 [4, 2, 1024, 2048], P('pipe', None, 'seq'), may hold values from -120 to 120
- keys: bfloat16 [4, 2, 1024, 512], P('pipe', None, 'seq'), may hold values from -5 to 5
- values: bfloat16 [4, 2, 1024, 512], P('pipe', None, 'seq'), may hold values from -6 to 6
- out_grad: bfloat16 [2, 1024, 2048], P(None, 'seq'), may hold values from -6 to 6
- segments: int32 [2, 1024], replicated, may hold values from 0 to 15, never falling along the last dimension, each value on 1 to 256 neighbouring positions
Outputs:
- query_grads: bfloat16 [4, 2, 1024, 2048], P('pipe', None, 'seq')
- key_grads: bfloat16 [4, 2, 1024, 512], P('pipe', None, 'seq')
- value_grads: bfloat16 [4, 2, 1024, 512], P('pipe', None, 'seq')
Inputs may be any that keep to these rules, and one draw needn't show every extreme that they name: `segments`: segment numbers never fall along a micro-batch.
All inputs are finite; a program needn't handle non-finite values.
Results may differ from a plain program's by a relative error of at most 0.014.
Values may be sent and summed in bfloat16 or wider, within the bound.
A program may use at most 64 MiB of HBM per device.

v0:
```python
import jax
import jax.numpy as jnp
from jax import lax
from jax.sharding import PartitionSpec as P

DH = 128
WINDOW = 128


def from_behind(block, axis, distance):
    devices = range(lax.axis_size(axis))
    route = [(i - distance, i) for i in devices if i - distance in devices]
    return lax.ppermute(block, axis, route)


def tile_backward(query, key_rows, value_rows, grad_out, allowed):
    row_count = query.shape[0]
    key_count = key_rows.shape[0]
    kv_heads = key_rows.shape[1] // DH
    group_size = query.shape[1] // (kv_heads * DH)
    score_scale = DH ** (-0.5)
    query_heads = query.reshape(row_count, kv_heads, group_size, DH)
    grad_heads = grad_out.reshape(row_count, kv_heads, group_size, DH)
    key_heads = key_rows.reshape(key_count, kv_heads, DH)
    value_heads = value_rows.reshape(key_count, kv_heads, DH)
    scores = (
        jnp.einsum("qhgd,khd->hgqk", query_heads, key_heads, preferred_element_type=jnp.float32)
        * score_scale
    )
    masked = jnp.where(allowed, scores, -jnp.inf)
    row_max = jnp.max(masked, axis=-1, keepdims=True)
    weights = jnp.exp(masked - row_max)
    probability = weights / jnp.sum(weights, axis=-1, keepdims=True)
    prob_low = probability.astype(jnp.bfloat16)
    output = jnp.einsum("hgqk,khd->qhgd", prob_low, value_heads, preferred_element_type=jnp.float32)
    grad_prob = jnp.einsum(
        "qhgd,khd->hgqk", grad_heads, value_heads, preferred_element_type=jnp.float32
    )
    grad_dot = jnp.transpose(jnp.sum(grad_heads.astype(jnp.float32) * output, axis=-1), (1, 2, 0))[
        ..., None
    ]
    grad_score = (probability * (grad_prob - grad_dot)).astype(jnp.bfloat16)
    query_grad = (
        jnp.einsum("hgqk,khd->qhgd", grad_score, key_heads, preferred_element_type=jnp.float32)
        * score_scale
    )
    key_grad = (
        jnp.einsum("hgqk,qhgd->khd", grad_score, query_heads, preferred_element_type=jnp.float32)
        * score_scale
    )
    value_grad = jnp.einsum(
        "hgqk,qhgd->khd", prob_low, grad_heads, preferred_element_type=jnp.float32
    )
    return (
        query_grad.reshape(row_count, -1),
        key_grad.reshape(key_count, -1),
        value_grad.reshape(key_count, -1),
    )


def item_backward(query, key_rows, value_rows, grad_out, allowed):
    return tile_backward(query, key_rows, value_rows, grad_out, allowed)


def per_device(queries, keys, values, out_grad, segments):
    micro_count = queries.shape[1]
    row_count = queries.shape[2]
    query_width = queries.shape[3]
    key_width = keys.shape[3]
    section_count = lax.axis_size("pipe")
    section_index = lax.axis_index("pipe")
    seq_index = lax.axis_index("seq")
    own_query = queries[0]
    own_key = keys[0]
    own_value = values[0]
    seg_padded = jnp.concatenate(
        [jnp.full((micro_count, row_count), -1, jnp.int32), segments], axis=1
    )
    query_pos = seq_index * row_count + jnp.arange(row_count, dtype=jnp.int32)
    key_pos = seq_index * row_count - row_count + jnp.arange(2 * row_count, dtype=jnp.int32)
    seg_query = lax.dynamic_slice_in_dim(
        seg_padded, seq_index * row_count + row_count, row_count, axis=1
    )
    seg_key = lax.dynamic_slice_in_dim(seg_padded, seq_index * row_count, 2 * row_count, axis=1)
    near = (
        (key_pos[None, :] <= query_pos[:, None])
        & (query_pos[:, None] - key_pos[None, :] < WINDOW)
        & (key_pos[None, :] >= 0)
    )
    masks = near[None] & (seg_query[:, :, None] == seg_key[:, None, :])
    halo_key, halo_value = from_behind((own_key, own_value), "seq", 1)
    key_rows = jnp.concatenate([halo_key, own_key], axis=1)
    value_rows = jnp.concatenate([halo_value, own_value], axis=1)
    pieces = 1

    def pass_back(sent_grad):
        return from_behind(sent_grad, "pipe", -1)

    item_count = micro_count * pieces
    tick_count = item_count + section_count - 1
    piece_query = query_width // pieces
    piece_key = key_width // pieces

    def tick(tick_step, state_carry):
        sent_grad, query_all, key_all, value_all = state_carry
        incoming = pass_back(sent_grad)
        item_index = tick_step - (section_count - 1 - section_index)
        valid = (item_index >= 0) & (item_index < item_count)
        safe_item = jnp.clip(item_index, 0, item_count - 1)
        batch_index = safe_item // pieces
        half_index = safe_item % pieces

        def do_work(unused):
            query = lax.dynamic_slice(
                own_query, (batch_index, 0, half_index * piece_query), (1, row_count, piece_query)
            )[0]
            key_piece = lax.dynamic_slice(
                key_rows, (batch_index, 0, half_index * piece_key), (1, 2 * row_count, piece_key)
            )[0]
            value_piece = lax.dynamic_slice(
                value_rows, (batch_index, 0, half_index * piece_key), (1, 2 * row_count, piece_key)
            )[0]
            top_grad = lax.dynamic_slice(
                out_grad, (batch_index, 0, half_index * piece_query), (1, row_count, piece_query)
            )[0]
            grad_in = jnp.where(section_index == section_count - 1, top_grad, incoming)
            allowed = lax.dynamic_index_in_dim(masks, batch_index, 0, keepdims=False)
            query_grad, key_grad, value_grad = item_backward(
                query, key_piece, value_piece, grad_in, allowed
            )
            grad_next = (grad_in.astype(jnp.float32) + query_grad).astype(jnp.bfloat16)
            query_new = lax.dynamic_update_slice(
                query_all, grad_next[None], (batch_index, 0, half_index * piece_query)
            )
            key_new = lax.dynamic_update_slice(
                key_all, key_grad[None], (batch_index, 0, half_index * piece_key)
            )
            value_new = lax.dynamic_update_slice(
                value_all, value_grad[None], (batch_index, 0, half_index * piece_key)
            )
            return (grad_next, query_new, key_new, value_new)

        def keep_carry(unused):
            return (sent_grad, query_all, key_all, value_all)

        return lax.cond(valid, do_work, keep_carry, 0)

    start_state = (
        jnp.zeros((row_count, piece_query), jnp.bfloat16),
        jnp.zeros((micro_count, row_count, query_width), jnp.bfloat16),
        jnp.zeros((micro_count, 2 * row_count, key_width), jnp.float32),
        jnp.zeros((micro_count, 2 * row_count, key_width), jnp.float32),
    )
    sent_grad, query_all, key_all, value_all = lax.fori_loop(0, tick_count, tick, start_state)
    back_key, back_value = from_behind(
        (key_all[:, :row_count], value_all[:, :row_count]), "seq", -1
    )
    key_grads = (key_all[:, row_count:] + back_key).astype(jnp.bfloat16)
    value_grads = (value_all[:, row_count:] + back_value).astype(jnp.bfloat16)
    return (query_all[None], key_grads[None], value_grads[None])


def solution(mesh):
    placed = (
        P("pipe", None, "seq", None),
        P("pipe", None, "seq", None),
        P("pipe", None, "seq", None),
        P(None, "seq", None),
        P(),
    )
    return jax.shard_map(
        per_device,
        mesh=mesh,
        in_specs=placed,
        out_specs=(
            P("pipe", None, "seq", None),
            P("pipe", None, "seq", None),
            P("pipe", None, "seq", None),
        ),
        check_vma=False,
    )
```

profile of v0, /device:TPU:1, one launch (start us, length us, event | category | flops | bytes accessed | tf_op | source)
XLA Modules:
  0.0 163.4 jit_solution(12518245372410041005)
XLA Ops:
  1.9 4.6 %collective-permute-start.2 = (bf16[2,128,512]{1,2,0:T(8,128)(2,1)S(1)}, bf16[2,128,512]{1,2,0:T(8,128)(2,1)S(1)}, u32[]{:S(2)}, u32[]{:S(2)}) collective-permute-start(bf16[2,128,512]{1,2,0:T(8,128)(2,1)S(1)} %bitcast.98), channel_id=1, source_target_pairs={{0,1},{1,2},{2,3},{3,4},{4,5},{5,6},{6,7},{8,9},{9,10},{10,11},{11... | collective-permute-start | bytes 786440 | tf_op jit(solution)/shard_map/ppermute | solution.py:13
  7.6 1.9 %collective-permute-start.1 = (bf16[2,128,512]{1,2,0:T(8,128)(2,1)S(1)}, bf16[2,128,512]{1,2,0:T(8,128)(2,1)S(1)}, u32[]{:S(2)}, u32[]{:S(2)}) collective-permute-start(bf16[2,128,512]{1,2,0:T(8,128)(2,1)S(1)} %bitcast.96), channel_id=1, source_target_pairs={{0,1},{1,2},{2,3},{3,4},{4,5},{5,6},{6,7},{8,9},{9,10},{10,11},{11... | collective-permute-start | bytes 786440 | tf_op jit(solution)/shard_map/ppermute | solution.py:13
  10.4 2.3 %copy.31 = bf16[1,2,128,2048]{2,3,1,0:T(8,128)(2,1)} copy(bf16[1,2,128,2048]{3,2,1,0:T(8,128)(2,1)} %param.9) | data formatting | bytes 2097152 | tf_op args[0]
  12.7 1.3 copy.33
  19.0 121.3 %while.22 = (s32[]{:T(128)}, bf16[128,2048]{0,1:T(8,128)(2,1)S(1)}, bf16[2,128,2048]{1,2,0:T(8,128)(2,1)}, f32[2,256,512]{1,2,0:T(8,128)}, f32[2,256,512]{1,2,0:...) while((s32[]{:T(128)}, bf16[128,2048]{0,1:T(8,128)(2,1)S(1)}, ...), condition=%wide.region_6.7_spmd.clone, body=%wide.region_0.6_spmd.clone.sunk | while | flops 812841216 | bytes 32125980 | solution.py:154
  20.3 13.6 %collective-permute-done = bf16[128,2048]{0,1:T(8,128)(2,1)S(1)} collective-permute-done((bf16[128,2048]{0,1:T(8,128)(2,1)S(1)}, bf16[128,2048]{0,1:T(8,128)(2,1)S(1)}, u32[]{:S(2)}, u32[]{:S(2)}) %collective-permute-start) | collective-permute-done | bytes 524320 | tf_op jit(solution)/shard_map/while/body/eval_jaxpr/ppermute | solution.py:13
  33.9 1.3 collective-permute-start
  35.2 13.6 %collective-permute-done = bf16[128,2048]{0,1:T(8,128)(2,1)S(1)} collective-permute-done((bf16[128,2048]{0,1:T(8,128)(2,1)S(1)}, bf16[128,2048]{0,1:T(8,128)(2,1)S(1)}, u32[]{:S(2)}, u32[]{:S(2)}) %collective-permute-start) | collective-permute-done | bytes 524320 | tf_op jit(solution)/shard_map/while/body/eval_jaxpr/ppermute | solution.py:13
  48.8 1.3 collective-permute-start
  50.1 12.6 %collective-permute-done = bf16[128,2048]{0,1:T(8,128)(2,1)S(1)} collective-permute-done((bf16[128,2048]{0,1:T(8,128)(2,1)S(1)}, bf16[128,2048]{0,1:T(8,128)(2,1)S(1)}, u32[]{:S(2)}, u32[]{:S(2)}) %collective-permute-start) | collective-permute-done | bytes 524320 | tf_op jit(solution)/shard_map/while/body/eval_jaxpr/ppermute | solution.py:13
  62.7 1.3 collective-permute-start
  64.0 41.1 %collective-permute-done = bf16[128,2048]{0,1:T(8,128)(2,1)S(1)} collective-permute-done((bf16[128,2048]{0,1:T(8,128)(2,1)S(1)}, bf16[128,2048]{0,1:T(8,128)(2,1)S(1)}, u32[]{:S(2)}, u32[]{:S(2)}) %collective-permute-start) | collective-permute-done | bytes 524320 | tf_op jit(solution)/shard_map/while/body/eval_jaxpr/ppermute | solution.py:13
  105.1 11.3 %conditional.3 = ((bf16[128,2048]{0,1:T(8,128)(2,1)S(1)}, bf16[2,128,2048]{1,2,0:T(8,128)(2,1)}, f32[2,256,512]{1,2,0:T(8,128)}, f32[2,256,512]{1,2,0:T(8,128)})) conditional(s32[]{:T(128)} %convert_element_type.61, (bf16[128,2048]{0,1:T(8,128)(2,1)S(1)}, bf16[2,128,2048]{1,2,0:T(8,128)(2,1)}, f32[2,256,512]{1,2,0:T(8,128)}, ...), branch_computations={%region_1.1_spmd, %region_2.5_spmd} | conditional | flops 812841216 | bytes 30028450 | solution.py:146
  107.3 1.7 %constant_dynamic-slice_fusion.1 = bf16[1,256,512]{1,2,0:T(8,128)(2,1)} fusion(bf16[2,256,512]{1,2,0:T(8,128)(2,1)} %get-tuple-element.406, s32[]{:T(128)S(6)} %min.13), kind=kLoop, calls=%fused_computation.28 | loop fusion | bytes 524292 | tf_op jit(solution)/shard_map/while/body/eval_jaxpr/cond/branch_1_fun/dynamic_slice | solution.py:120
  117.6 11.4 %collective-permute-done = bf16[128,2048]{0,1:T(8,128)(2,1)S(1)} collective-permute-done((bf16[128,2048]{0,1:T(8,128)(2,1)S(1)}, bf16[128,2048]{0,1:T(8,128)(2,1)S(1)}, u32[]{:S(2)}, u32[]{:S(2)}) %collective-permute-start) | collective-permute-done | bytes 524320 | tf_op jit(solution)/shard_map/while/body/eval_jaxpr/ppermute | solution.py:13
  129.0 11.3 %conditional.3 = ((bf16[128,2048]{0,1:T(8,128)(2,1)S(1)}, bf16[2,128,2048]{1,2,0:T(8,128)(2,1)}, f32[2,256,512]{1,2,0:T(8,128)}, f32[2,256,512]{1,2,0:T(8,128)})) conditional(s32[]{:T(128)} %convert_element_type.61, (bf16[128,2048]{0,1:T(8,128)(2,1)S(1)}, bf16[2,128,2048]{1,2,0:T(8,128)(2,1)}, f32[2,256,512]{1,2,0:T(8,128)}, ...), branch_computations={%region_1.1_spmd, %region_2.5_spmd} | conditional | flops 812841216 | bytes 30028450 | solution.py:146
  131.2 1.7 %constant_dynamic-slice_fusion.1 = bf16[1,256,512]{1,2,0:T(8,128)(2,1)} fusion(bf16[2,256,512]{1,2,0:T(8,128)(2,1)} %get-tuple-element.406, s32[]{:T(128)S(6)} %min.13), kind=kLoop, calls=%fused_computation.28 | loop fusion | bytes 524292 | tf_op jit(solution)/shard_map/while/body/eval_jaxpr/cond/branch_1_fun/dynamic_slice | solution.py:120
  140.3 1.6 copy.35
  142.7 6.1 %collective-permute-start.3 = (f32[2,128,512]{2,1,0:T(8,128)}, f32[2,128,512]{2,1,0:T(8,128)S(1)}, u32[]{:S(2)}, u32[]{:S(2)}) collective-permute-start(f32[2,128,512]{2,1,0:T(8,128)} %slice.17), channel_id=1, source_target_pairs={{1,0},{2,1},{3,2},{4,3},{5,4},{6,5},{7,6},{9,8},{10,9},{11,10},{12... | collective-permute-start | bytes 1572872 | tf_op jit(solution)/shard_map/ppermute | solution.py:13
  148.8 1.6 copy.37
  151.2 1.9 %collective-permute-start.4 = (f32[2,128,512]{2,1,0:T(8,128)}, f32[2,128,512]{2,1,0:T(8,128)S(1)}, u32[]{:S(2)}, u32[]{:S(2)}) collective-permute-start(f32[2,128,512]{2,1,0:T(8,128)} %slice.19), channel_id=1, source_target_pairs={{1,0},{2,1},{3,2},{4,3},{5,4},{6,5},{7,6},{9,8},{10,9},{11,10},{12... | collective-permute-start | bytes 1572872 | tf_op jit(solution)/shard_map/ppermute | solution.py:13
  153.1 2.3 %copy.34 = bf16[2,128,2048]{2,1,0:T(8,128)(2,1)} copy(bf16[2,128,2048]{1,2,0:T(8,128)(2,1)} %get-tuple-element.433) | data formatting | bytes 2097152 | tf_op jit(solution)/shard_map/while | solution.py:154
  155.4 1.7 %collective-permute-done.3 = f32[2,128,512]{2,1,0:T(8,128)S(1)} collective-permute-done((f32[2,128,512]{2,1,0:T(8,128)}, f32[2,128,512]{2,1,0:T(8,128)S(1)}, u32[]{:S(2)}, u32[]{:S(2)}) %collective-permute-start.3) | collective-permute-done | bytes 524320 | tf_op jit(solution)/shard_map/ppermute | solution.py:13
  157.8 4.8 %collective-permute-done.4 = f32[2,128,512]{2,1,0:T(8,128)S(1)} collective-permute-done((f32[2,128,512]{2,1,0:T(8,128)}, f32[2,128,512]{2,1,0:T(8,128)S(1)}, u32[]{:S(2)}, u32[]{:S(2)}) %collective-permute-start.4) | collective-permute-done | bytes 524320 | tf_op jit(solution)/shard_map/ppermute | solution.py:13
  (67 shorter events, 33.0 us)
Async XLA Ops:
  0.6 12.1 %copy-start.1 = (bf16[2,128,2048]{2,1,0:T(8,128)(2,1)S(1)}, bf16[2,128,2048]{2,1,0:T(8,128)(2,1)}, u32[]{:S(2)}) copy-start(bf16[2,128,2048]{2,1,0:T(8,128)(2,1)} %param.12) | copy-start | bytes 3145732
  1.9 12.1 %collective-permute-start.2 = (bf16[2,128,512]{1,2,0:T(8,128)(2,1)S(1)}, bf16[2,128,512]{1,2,0:T(8,128)(2,1)S(1)}, u32[]{:S(2)}, u32[]{:S(2)}) collective-permute-start(bf16[2,128,512]{1,2,0:T(8,128)(2,1)S(1)} %bitcast.98), channel_id=1, source_target_pairs={{0,1},{1,2},{2,3},{3,4},{4,5},{5,6},{6,7},{8,9},{9,10},{10,11},{11... | collective-permute-start | bytes 786440 | tf_op jit(solution)/shard_map/ppermute | solution.py:13
  7.6 7.3 %collective-permute-start.1 = (bf16[2,128,512]{1,2,0:T(8,128)(2,1)S(1)}, bf16[2,128,512]{1,2,0:T(8,128)(2,1)S(1)}, u32[]{:S(2)}, u32[]{:S(2)}) collective-permute-start(bf16[2,128,512]{1,2,0:T(8,128)(2,1)S(1)} %bitcast.96), channel_id=1, source_target_pairs={{0,1},{1,2},{2,3},{3,4},{4,5},{5,6},{6,7},{8,9},{9,10},{10,11},{11... | collective-permute-start | bytes 786440 | tf_op jit(solution)/shard_map/ppermute | solution.py:13
  10.4 3.6 %copy-start.3 = (s32[2,1024]{1,0:T(2,128)S(1)}, s32[2,1024]{1,0:T(2,128)}, u32[]{:S(2)}) copy-start(s32[2,1024]{1,0:T(2,128)} %param.13) | copy-start | bytes 24580
  19.0 14.9 %collective-permute-start = (bf16[128,2048]{0,1:T(8,128)(2,1)S(1)}, bf16[128,2048]{0,1:T(8,128)(2,1)S(1)}, u32[]{:S(2)}, u32[]{:S(2)}) collective-permute-start(bf16[128,2048]{0,1:T(8,128)(2,1)S(1)} %get-tuple-element.661), channel_id=1, source_target_pairs={{8,0},{16,8},{24,16},{9,1},{17,9},{25,17},{10,2},{18,10},{26,18},{... | collective-permute-start | bytes 1572872 | tf_op jit(solution)/shard_map/while/body/eval_jaxpr/ppermute | solution.py:13
  33.9 14.9 %collective-permute-start = (bf16[128,2048]{0,1:T(8,128)(2,1)S(1)}, bf16[128,2048]{0,1:T(8,128)(2,1)S(1)}, u32[]{:S(2)}, u32[]{:S(2)}) collective-permute-start(bf16[128,2048]{0,1:T(8,128)(2,1)S(1)} %get-tuple-element.661), channel_id=1, source_target_pairs={{8,0},{16,8},{24,16},{9,1},{17,9},{25,17},{10,2},{18,10},{26,18},{... | collective-permute-start | bytes 1572872 | tf_op jit(solution)/shard_map/while/body/eval_jaxpr/ppermute | solution.py:13
  48.8 13.9 %collective-permute-start = (bf16[128,2048]{0,1:T(8,128)(2,1)S(1)}, bf16[128,2048]{0,1:T(8,128)(2,1)S(1)}, u32[]{:S(2)}, u32[]{:S(2)}) collective-permute-start(bf16[128,2048]{0,1:T(8,128)(2,1)S(1)} %get-tuple-element.661), channel_id=1, source_target_pairs={{8,0},{16,8},{24,16},{9,1},{17,9},{25,17},{10,2},{18,10},{26,18},{... | collective-permute-start | bytes 1572872 | tf_op jit(solution)/shard_map/while/body/eval_jaxpr/ppermute | solution.py:13
  62.7 42.4 %collective-permute-start = (bf16[128,2048]{0,1:T(8,128)(2,1)S(1)}, bf16[128,2048]{0,1:T(8,128)(2,1)S(1)}, u32[]{:S(2)}, u32[]{:S(2)}) collective-permute-start(bf16[128,2048]{0,1:T(8,128)(2,1)S(1)} %get-tuple-element.661), channel_id=1, source_target_pairs={{8,0},{16,8},{24,16},{9,1},{17,9},{25,17},{10,2},{18,10},{26,18},{... | collective-permute-start | bytes 1572872 | tf_op jit(solution)/shard_map/while/body/eval_jaxpr/ppermute | solution.py:13
  110.9 1.0 copy-start
  115.1 1.2 copy-start.2
  116.3 12.7 %collective-permute-start = (bf16[128,2048]{0,1:T(8,128)(2,1)S(1)}, bf16[128,2048]{0,1:T(8,128)(2,1)S(1)}, u32[]{:S(2)}, u32[]{:S(2)}) collective-permute-start(bf16[128,2048]{0,1:T(8,128)(2,1)S(1)} %get-tuple-element.661), channel_id=1, source_target_pairs={{8,0},{16,8},{24,16},{9,1},{17,9},{25,17},{10,2},{18,10},{26,18},{... | collective-permute-start | bytes 1572872 | tf_op jit(solution)/shard_map/while/body/eval_jaxpr/ppermute | solution.py:13
  134.8 1.0 copy-start
  139.1 1.2 copy-start.2
  142.7 14.4 %collective-permute-start.3 = (f32[2,128,512]{2,1,0:T(8,128)}, f32[2,128,512]{2,1,0:T(8,128)S(1)}, u32[]{:S(2)}, u32[]{:S(2)}) collective-permute-start(f32[2,128,512]{2,1,0:T(8,128)} %slice.17), channel_id=1, source_target_pairs={{1,0},{2,1},{3,2},{4,3},{5,4},{6,5},{7,6},{9,8},{10,9},{11,10},{12... | collective-permute-start | bytes 1572872 | tf_op jit(solution)/shard_map/ppermute | solution.py:13
  151.2 11.5 %collective-permute-start.4 = (f32[2,128,512]{2,1,0:T(8,128)}, f32[2,128,512]{2,1,0:T(8,128)S(1)}, u32[]{:S(2)}, u32[]{:S(2)}) collective-permute-start(f32[2,128,512]{2,1,0:T(8,128)} %slice.19), channel_id=1, source_target_pairs={{1,0},{2,1},{3,2},{4,3},{5,4},{6,5},{7,6},{9,8},{10,9},{11,10},{12... | collective-permute-start | bytes 1572872 | tf_op jit(solution)/shard_map/ppermute | solution.py:13
where the time goes:
time: 164 us; the launch traced here: 163 us
  waiting for transfers between devices  98.8 us (60%)
  local copies, waits for them, and re-layouts  28.2 us (17%)
  starting transfers between devices  20.9 us (13%)
  other arithmetic  8.63 us (5%)
  matrix products  5.9 us (4%)
    ppermute x9, waiting for transfers between devices, from_behind(): return lax.ppermute(block, axis, route)  98.8 us
    ppermute x9, starting transfers between devices, from_behind(): return lax.ppermute(block, axis, route)  20.9 us
    unnamed x8, local copies, waits for them, and re-layouts  5.92 us
    while x3, local copies, waits for them, and re-layouts, per_device(): lax.fori_loop(0, tick_count, tick, start_state)  5.38 us
    dynamic_slice x2, local copies, waits for them, and re-layouts, do_work(): lax.dynamic_slice(value_rows, (batch_index, 0, half_index * piece_key), (...  3.35 us
  transfers between devices with their start and end apart: 9, of which 7 were waited for; matrix products, arithmetic and copies ran while one was open for 7% of the time, Pallas kernels for 0%

commit v1 on v0

v1 whole, which is shorter than its diff:
```python
import functools

import jax
import jax.numpy as jnp
from jax import lax
from jax.experimental import pallas as pl
from jax.experimental.pallas import tpu as pltpu
from jax.sharding import PartitionSpec as P

DH = 128
LOG2E = 1.4426950408889634
MESH = pl.DeviceIdType.MESH
CHUNK = 2

NT = (((1,), (1,)), ((), ()))
TN = (((0,), (0,)), ((), ()))
NN = (((1,), (0,)), ((), ()))


def dot(left, right, dims):
    return lax.dot_general(left, right, dims, preferred_element_type=jnp.float32)


def stack_heads(rows):
    count = rows.shape[1] // DH
    return jnp.concatenate([rows[:, i * DH : (i + 1) * DH] for i in range(count)], axis=0)


def kernel(
    sections,
    seq_size,
    kv_heads,
    group,
    q_hbm,
    k_hbm,
    v_hbm,
    g_hbm,
    seg_ref,
    qg_hbm,
    kg_hbm,
    vg_hbm,
    x_buf,
    kv_buf,
    prob_buf,
    g_in,
    g_out,
    part_own,
    part_send,
    part_recv,
    kv_out,
    bias_ref,
    pick_ref,
    x_sem,
    own_sem,
    halo_send,
    halo_recv,
    g_send,
    g_recv,
    part_send_sem,
    part_recv_sem,
    qg_sem,
    kvg_sem,
):
    section = lax.axis_index("pipe")
    block = lax.axis_index("seq")
    micro = q_hbm.shape[1]
    items = micro * kv_heads
    per_item = group // CHUNK
    wide = CHUNK * DH
    scale = DH**-0.5
    last = section == sections - 1
    has_next = section > 0
    has_left = block > 0
    has_right = block < seq_size - 1

    def place(item):
        return item // kv_heads, pl.multiple_of(lax.rem(item, kv_heads) * DH, DH)

    def loop(count, body):
        def step(i, carry):
            body(i)
            return carry

        lax.fori_loop(0, count, step, 0)

    def own_copies(item):
        b, col = place(item)
        return (
            pltpu.make_async_copy(
                k_hbm.at[0, b, :, pl.ds(col, DH)], kv_buf.at[item, 0, 1], own_sem.at[item, 0]
            ),
            pltpu.make_async_copy(
                v_hbm.at[0, b, :, pl.ds(col, DH)], kv_buf.at[item, 1, 1], own_sem.at[item, 1]
            ),
            pltpu.make_async_copy(
                q_hbm.at[0, b, :, pl.ds(pl.multiple_of(col * group, DH), group * DH)],
                x_buf.at[item],
                x_sem.at[item],
            ),
        )

    def halo_copies(item):
        b, col = place(item)
        return tuple(
            pltpu.make_async_remote_copy(
                src_ref=ref.at[0, b, :, pl.ds(col, DH)],
                dst_ref=kv_buf.at[item, i, 0],
                send_sem=halo_send.at[item, i],
                recv_sem=halo_recv.at[item, i],
                device_id=(section, block + 1),
                device_id_type=MESH,
            )
            for i, ref in enumerate((k_hbm, v_hbm))
        )

    def grad_copy(chunk):
        return pltpu.make_async_remote_copy(
            src_ref=g_out.at[chunk],
            dst_ref=g_in.at[chunk],
            send_sem=g_send.at[chunk],
            recv_sem=g_recv.at[chunk],
            device_id=(section - 1, block),
            device_id_type=MESH,
        )

    def top_copy(chunk):
        per_micro = kv_heads * per_item
        col = pl.multiple_of(lax.rem(chunk, per_micro) * wide, DH)
        return pltpu.make_async_copy(
            g_hbm.at[chunk // per_micro, :, pl.ds(col, wide)], g_in.at[chunk], g_recv.at[chunk]
        )

    def out_copy(chunk):
        per_micro = kv_heads * per_item
        col = pl.multiple_of(lax.rem(chunk, per_micro) * wide, DH)
        return pltpu.make_async_copy(
            g_out.at[chunk],
            qg_hbm.at[0, chunk // per_micro, :, pl.ds(col, wide)],
            qg_sem.at[chunk],
        )

    def part_copy(item):
        return pltpu.make_async_remote_copy(
            src_ref=part_send.at[item],
            dst_ref=part_recv.at[item],
            send_sem=part_send_sem.at[item],
            recv_sem=part_recv_sem.at[item],
            device_id=(section, block - 1),
            device_id_type=MESH,
        )

    def kv_out_copies(item):
        b, col = place(item)
        return tuple(
            pltpu.make_async_copy(
                kv_out.at[item, i], ref.at[0, b, :, pl.ds(col, DH)], kvg_sem.at[item, i]
            )
            for i, ref in enumerate((kg_hbm, vg_hbm))
        )

    barrier = pltpu.get_barrier_semaphore()
    neighbours = (
        (has_next, (section - 1, block)),
        (section < sections - 1, (section + 1, block)),
        (has_left, (section, block - 1)),
        (has_right, (section, block + 1)),
    )
    for exists, device in neighbours:

        @pl.when(exists)
        def _(device=device):
            pl.semaphore_signal(barrier, inc=1, device_id=device, device_id_type=MESH)

    def start_own(item):
        for copy in own_copies(item):
            copy.start()

    loop(items, start_own)

    @pl.when(last)
    def _():
        loop(items * per_item, lambda chunk: top_copy(chunk).start())

    @pl.when(jnp.logical_not(has_left))
    def _():
        def clear(item):
            for i in range(2):
                kv_buf[item, i, 0] = jnp.zeros((DH, DH), jnp.bfloat16)

        loop(items, clear)

    @pl.when(jnp.logical_not(has_right))
    def _():
        def clear(item):
            part_recv[item] = jnp.zeros(part_recv.shape[1:], jnp.bfloat16)

        loop(items, clear)

    key_at = lax.broadcasted_iota(jnp.int32, (DH, DH), 0)
    query_at = lax.broadcasted_iota(jnp.int32, (DH, DH), 1)
    in_own = key_at <= query_at
    before = jnp.maximum(block - 1, 0)
    for b in range(micro):
        seg_query = seg_ref[b : b + 1, pl.ds(pl.multiple_of(block * DH, DH), DH)]
        seg_halo = seg_ref[b : b + 1, pl.ds(pl.multiple_of(before * DH, DH), DH)]
        seg_query = jnp.broadcast_to(seg_query.astype(jnp.float32), (DH, DH))
        seg_halo = jnp.broadcast_to(seg_halo.astype(jnp.float32), (DH, DH))
        seg_halo = jnp.where(has_left, seg_halo, -1.0)
        seg_key = jnp.where(in_own, seg_query.T, seg_halo.T)
        bias_ref[b] = jnp.where(seg_key == seg_query, 0.0, -1e30)
    pick_ref[0] = jnp.where(in_own, 0.0, 1.0).astype(jnp.bfloat16)
    pick_ref[1] = jnp.where(in_own, 1.0, 0.0).astype(jnp.bfloat16)

    pl.semaphore_wait(barrier, sum(exists.astype(jnp.int32) for exists, _ in neighbours))

    @pl.when(has_right)
    def _():
        def send_halo(item):
            for copy in halo_copies(item):
                copy.start()

        loop(items, send_halo)

    def merge(both):
        count = both.shape[1] // DH
        keep = jnp.concatenate([in_own] * count, axis=1)
        return jnp.where(keep, both[DH:], both[:DH])

    def spread(packed):
        count = packed.shape[1] // DH
        return jnp.concatenate(
            [jnp.concatenate([pick_ref[i]] * count, axis=1) * packed for i in range(2)], axis=0
        )

    def probabilities(item):
        for copy in own_copies(item):
            copy.wait()

        @pl.when(has_left)
        def _():
            for copy in halo_copies(item):
                copy.wait_recv()

        key = kv_buf[item, 0].reshape(2 * DH, DH)
        bias = bias_ref[item // kv_heads]
        for part in range(per_item):
            cols = slice(part * wide, (part + 1) * wide)
            query = stack_heads(x_buf[item, :, cols])
            score = merge(dot(key, query, NT)) + jnp.concatenate([bias] * CHUNK, axis=1)
            top = jnp.max(score, axis=0, keepdims=True)
            weight = jnp.exp2((score - top) * (scale * LOG2E))
            total = jnp.sum(weight, axis=0, keepdims=True)
            prob_buf[item, :, cols] = weight * (1.0 / total)

    @pl.when(jnp.logical_not(last))
    def _():
        loop(items, probabilities)

    def backward(item):
        @pl.when(last)
        def _():
            probabilities(item)

        key = kv_buf[item, 0].reshape(2 * DH, DH)
        value = kv_buf[item, 1].reshape(2 * DH, DH)
        key_grad = value_grad = None
        for part in range(per_item):
            chunk = item * per_item + part
            pltpu.make_async_copy(g_in.at[chunk], g_in.at[chunk], g_recv.at[chunk]).wait()
            cols = slice(part * wide, (part + 1) * wide)
            query = stack_heads(x_buf[item, :, cols])
            grad = stack_heads(g_in[chunk])
            prob = prob_buf[item, :, cols]
            prob_low = prob.astype(jnp.bfloat16)
            grad_prob = merge(dot(value, grad, NT))
            delta = jnp.sum(prob_low.astype(jnp.float32) * grad_prob, axis=0, keepdims=True)
            grad_score = spread((prob * (grad_prob - delta)).astype(jnp.bfloat16))
            query_grad = dot(grad_score, key, TN) * scale
            grad_next = (grad.astype(jnp.float32) + query_grad).astype(jnp.bfloat16)
            for i in range(CHUNK):
                g_out[chunk, :, i * DH : (i + 1) * DH] = grad_next[i * DH : (i + 1) * DH]

            @pl.when(has_next)
            def _():
                grad_copy(chunk).start()

            out_copy(chunk).start()
            key_part = dot(grad_score, query, NN)
            value_part = dot(spread(prob_low), grad, NN)
            key_grad = key_part if part == 0 else key_grad + key_part
            value_grad = value_part if part == 0 else value_grad + value_part
        for i, total in enumerate((key_grad * scale, value_grad)):
            part_send[item, i] = total[:DH].astype(jnp.bfloat16)
            part_own[item, i] = total[DH:]

        @pl.when(has_left)
        def _():
            part_copy(item).start()

    loop(items, backward)

    def finish(item):
        @pl.when(has_right)
        def _():
            part_copy(item).wait_recv()

        total = part_own[item] + part_recv[item].astype(jnp.float32)
        kv_out[item] = total.astype(jnp.bfloat16)
        for copy in kv_out_copies(item):
            copy.start()

    loop(items, finish)

    def drain(item):
        for copy in kv_out_copies(item):
            copy.wait()
        for part in range(per_item):
            chunk = item * per_item + part
            out_copy(chunk).wait()

            @pl.when(has_next)
            def _():
                grad_copy(chunk).wait_send()

        @pl.when(has_right)
        def _():
            for copy in halo_copies(item):
                copy.wait_send()

        @pl.when(has_left)
        def _():
            part_copy(item).wait_send()

    loop(items, drain)


def per_device(sections, seq_size, queries, keys, values, out_grad, segments):
    micro, rows, query_width = queries.shape[1:]
    key_width = keys.shape[3]
    kv_heads = key_width // DH
    group = query_width // key_width
    items = micro * kv_heads
    chunks = items * group // CHUNK
    anywhere = pl.BlockSpec(memory_space=pl.ANY)
    low, full = jnp.bfloat16, jnp.float32
    dma = pltpu.SemaphoreType.DMA
    return pl.pallas_call(
        functools.partial(kernel, sections, seq_size, kv_heads, group),
        out_shape=(
            jax.ShapeDtypeStruct(queries.shape, low),
            jax.ShapeDtypeStruct(keys.shape, low),
            jax.ShapeDtypeStruct(values.shape, low),
        ),
        in_specs=[anywhere] * 4 + [pl.BlockSpec(memory_space=pltpu.VMEM)],
        out_specs=(anywhere,) * 3,
        scratch_shapes=[
            pltpu.VMEM((items, rows, group * DH), low),
            pltpu.VMEM((items, 2, 2, rows, DH), low),
            pltpu.VMEM((items, rows, group * DH), full),
            pltpu.VMEM((chunks, rows, CHUNK * DH), low),
            pltpu.VMEM((chunks, rows, CHUNK * DH), low),
            pltpu.VMEM((items, 2, rows, DH), full),
            pltpu.VMEM((items, 2, rows, DH), low),
            pltpu.VMEM((items, 2, rows, DH), low),
            pltpu.VMEM((items, 2, rows, DH), low),
            pltpu.VMEM((micro, DH, DH), full),
            pltpu.VMEM((2, DH, DH), low),
            dma((items,)),
            dma((items, 2)),
            dma((items, 2)),
            dma((items, 2)),
            dma((chunks,)),
            dma((chunks,)),
            dma((items,)),
            dma((items,)),
            dma((chunks,)),
            dma((items, 2)),
        ],
        compiler_params=pltpu.CompilerParams(
            collective_id=0, has_side_effects=True, vmem_limit_bytes=40 * 1024 * 1024
        ),
        cost_estimate=pl.CostEstimate(
            flops=10 * items * group * rows * 2 * rows * DH,
            bytes_accessed=6 * 1024 * 1024,
            transcendentals=items * group * rows * rows,
        ),
    )(queries, keys, values, out_grad, segments)


def solution(mesh):
    sizes = dict(mesh.shape)
    split = P("pipe", None, "seq", None)
    return jax.shard_map(
        functools.partial(per_device, sizes["pipe"], sizes["seq"]),
        mesh=mesh,
        in_specs=(split, split, split, P(None, "seq", None), P()),
        out_specs=(split, split, split),
        check_vma=False,
    )
```

time: 164 us -> 51.8 us (0.32)
  waiting for transfers between devices: 98.8 us -> 0 us
  Pallas kernels: 0 us -> 43.4 us
  starting transfers between devices: 20.9 us -> 0 us
  local copies, waits for them, and re-layouts: 28.2 us -> 7.41 us
  other arithmetic: 8.63 us -> 0 us
  matrix products: 5.9 us -> 0 us
    ppermute x9 -> x0, waiting for transfers between devices: 98.8 us -> none  [from_behind(): return lax.ppermute(block, axis, route)]
    pallas_call x0 -> x1, Pallas kernels: none -> 43.4 us  [per_device(): pl.pallas_call(functools.partial(kernel, sections, seq_size, kv_heads, gr...]
    ppermute x9 -> x0, starting transfers between devices: 20.9 us -> none  [from_behind(): return lax.ppermute(block, axis, route)]
    dynamic_slice x12 -> x0, local copies, waits for them, and re-layouts: 8.19 us -> none  [the longest x2 3.35 us: do_work(): lax.dynamic_slice(value_rows, (batch_index, 0, half_index * piece_key), (...]
    while x3 -> x0, local copies, waits for them, and re-layouts: 5.38 us -> none  [per_device(): lax.fori_loop(0, tick_count, tick, start_state)]
    dot_general x10 -> x0, matrix products: 4.24 us -> none  [the longest x2 1.04 us: tile_backward(): jnp.einsum('qhgd,khd->hgqk', grad_heads, value_heads, preferred_element_t...]
    dynamic_update_slice x2 -> x0, other arithmetic: 2.31 us -> none  [do_work(): lax.dynamic_update_slice(query_all, grad_next[None], (batch_index, 0, hal...]
    select_n x2 -> x0, other arithmetic: 2.2 us -> none  [do_work(): grad_in = jnp.where(section_index == section_count - 1, top_grad, incoming)]
  transfers between devices with their start and end apart: 9 -> 0, of which waited for: 7 -> 0; matrix products, arithmetic and copies ran while one was open for 7% -> 0% of each run, Pallas kernels for 0% -> 0%
where the time goes in v1:
time: 51.8 us; the launch traced here: 51.5 us
  Pallas kernels  43.4 us (84%)
  local copies, waits for them, and re-layouts  7.41 us (14%)
  between operations  0.65 us (1%)
    pallas_call x1, Pallas kernels, per_device(): pl.pallas_call(functools.partial(kernel, sections, seq_size, kv_heads, gr...  43.4 us
    unnamed x13, local copies, waits for them, and re-layouts  7.41 us

profile of v1, /device:TPU:1, one launch (start us, length us, event | category | flops | bytes accessed | tf_op | source)
XLA Modules:
  0.0 51.5 jit_solution(14271779657213201728)
XLA Ops:
  0.6 0.0 copy-start
  0.6 1.2 %copy-done = bf16[1,2,128,2048]{3,2,1,0:T(8,128)(2,1)S(1)} copy-done((bf16[1,2,128,2048]{3,2,1,0:T(8,128)(2,1)S(1)}, bf16[1,2,128,2048]{3,2,1,0:T(8,128)(2,1)}, u32[]{:S(2)}) %copy-start) | copy-done | bytes 1048600
  1.9 0.0 copy-start.1
  1.9 1.2 %copy-done.1 = bf16[2,128,2048]{2,1,0:T(8,128)(2,1)S(1)} copy-done((bf16[2,128,2048]{2,1,0:T(8,128)(2,1)S(1)}, bf16[2,128,2048]{2,1,0:T(8,128)(2,1)}, u32[]{:S(2)}) %copy-start.1) | copy-done | bytes 1048600
  3.1 0.0 copy-start.2
  3.1 0.9 %copy-done.2 = bf16[1,2,128,512]{3,2,1,0:T(8,128)(2,1)S(1)} copy-done((bf16[1,2,128,512]{3,2,1,0:T(8,128)(2,1)S(1)}, bf16[1,2,128,512]{3,2,1,0:T(8,128)(2,1)}, u32[]{:S(2)}) %copy-start.2) | copy-done | bytes 262168
  4.0 0.0 copy-start.3
  4.0 0.9 %copy-done.3 = bf16[1,2,128,512]{3,2,1,0:T(8,128)(2,1)S(1)} copy-done((bf16[1,2,128,512]{3,2,1,0:T(8,128)(2,1)S(1)}, bf16[1,2,128,512]{3,2,1,0:T(8,128)(2,1)}, u32[]{:S(2)}) %copy-start.3) | copy-done | bytes 262168
  5.0 0.0 copy-start.4
  5.0 0.7 %copy-done.4 = s32[2,1024]{1,0:T(2,128)S(1)} copy-done((s32[2,1024]{1,0:T(2,128)S(1)}, s32[2,1024]{1,0:T(2,128)}, u32[]{:S(2)}) %copy-start.4) | copy-done | bytes 8216
  5.7 43.4 %shard_map.76 = (bf16[1,2,128,2048]{3,2,1,0:T(8,128)(2,1)S(1)}, bf16[1,2,128,512]{3,2,1,0:T(8,128)(2,1)S(1)}, bf16[1,2,128,512]{3,2,1,0:T(8,128)(2,1)S(1)}) custom-call(bf16[1,2,128,2048]{3,2,1,0:T(8,128)(2,1)S(1)} %copy-done, bf16[1,2,128,512]{3,2,1,0:T(8,128)(2,1)S(1)} %copy-done.2, bf16[1,2,128,512]{3,2,1,0:T(8,128)(2,1)S(1)} %copy-done.3, ...), custom_call_target="tpu_custom_call" | custom-call | flops 1342177280 | bytes 6291456 | tf_op jit(solution)/shard_map/pallas_call | solution.py:347
  49.1 1.0 %copy.11 = bf16[1,2,128,2048]{3,2,1,0:T(8,128)(2,1)} copy(bf16[1,2,128,2048]{3,2,1,0:T(8,128)(2,1)S(1)} %get-tuple-element.6) | data formatting | bytes 2097152
  50.1 0.7 %copy.12 = bf16[1,2,128,512]{3,2,1,0:T(8,128)(2,1)} copy(bf16[1,2,128,512]{3,2,1,0:T(8,128)(2,1)S(1)} %get-tuple-element.7) | data formatting | bytes 524288
  50.8 0.7 %copy.13 = bf16[1,2,128,512]{3,2,1,0:T(8,128)(2,1)} copy(bf16[1,2,128,512]{3,2,1,0:T(8,128)(2,1)S(1)} %get-tuple-element.8) | data formatting | bytes 524288
Async XLA Ops:
  0.6 1.2 %copy-start = (bf16[1,2,128,2048]{3,2,1,0:T(8,128)(2,1)S(1)}, bf16[1,2,128,2048]{3,2,1,0:T(8,128)(2,1)}, u32[]{:S(2)}) copy-start(bf16[1,2,128,2048]{3,2,1,0:T(8,128)(2,1)} %q_hbm.1) | copy-start | bytes 3145732
  1.9 1.2 %copy-start.1 = (bf16[2,128,2048]{2,1,0:T(8,128)(2,1)S(1)}, bf16[2,128,2048]{2,1,0:T(8,128)(2,1)}, u32[]{:S(2)}) copy-start(bf16[2,128,2048]{2,1,0:T(8,128)(2,1)} %g_hbm.1) | copy-start | bytes 3145732
  3.1 0.9 %copy-start.2 = (bf16[1,2,128,512]{3,2,1,0:T(8,128)(2,1)S(1)}, bf16[1,2,128,512]{3,2,1,0:T(8,128)(2,1)}, u32[]{:S(2)}) copy-start(bf16[1,2,128,512]{3,2,1,0:T(8,128)(2,1)} %k_hbm.1) | copy-start | bytes 786436
  4.0 0.9 %copy-start.3 = (bf16[1,2,128,512]{3,2,1,0:T(8,128)(2,1)S(1)}, bf16[1,2,128,512]{3,2,1,0:T(8,128)(2,1)}, u32[]{:S(2)}) copy-start(bf16[1,2,128,512]{3,2,1,0:T(8,128)(2,1)} %v_hbm.1) | copy-start | bytes 786436
  5.0 0.7 %copy-start.4 = (s32[2,1024]{1,0:T(2,128)S(1)}, s32[2,1024]{1,0:T(2,128)}, u32[]{:S(2)}) copy-start(s32[2,1024]{1,0:T(2,128)} %seg_ref.1) | copy-start | bytes 24580

commit v2 on v1

--- a/solution.py
+++ b/solution.py
@@ -10,7 +10,7 @@
 DH = 128
 LOG2E = 1.4426950408889634
 MESH = pl.DeviceIdType.MESH
-CHUNK = 2
+CHUNK = 1
 
 NT = (((1,), (1,)), ((), ()))
 TN = (((0,), (0,)), ((), ()))
@@ -35,13 +35,14 @@
     k_hbm,
     v_hbm,
     g_hbm,
-    seg_ref,
+    seg_hbm,
     qg_hbm,
     kg_hbm,
     vg_hbm,
     x_buf,
     kv_buf,
     prob_buf,
+    ds_buf,
     g_in,
     g_out,
     part_own,
@@ -50,6 +51,8 @@
     kv_out,
     bias_ref,
     pick_ref,
+    seg_ref,
+    seg_sem,
     x_sem,
     own_sem,
     halo_send,
@@ -171,11 +174,24 @@
         def _(device=device):
             pl.semaphore_signal(barrier, inc=1, device_id=device, device_id_type=MESH)
 
+    seg_copy = pltpu.make_async_copy(seg_hbm, seg_ref, seg_sem)
+    seg_copy.start()
+
     def start_own(item):
         for copy in own_copies(item):
             copy.start()
 
     loop(items, start_own)
+
+    pl.semaphore_wait(barrier, sum(exists.astype(jnp.int32) for exists, _ in neighbours))
+
+    @pl.when(has_right)
+    def _():
+        def send_halo(item):
+            for copy in halo_copies(item):
+                copy.start()
+
+        loop(items, send_halo)
 
     @pl.when(last)
     def _():
@@ -200,6 +216,7 @@
     query_at = lax.broadcasted_iota(jnp.int32, (DH, DH), 1)
     in_own = key_at <= query_at
     before = jnp.maximum(block - 1, 0)
+    seg_copy.wait()
     for b in range(micro):
         seg_query = seg_ref[b : b + 1, pl.ds(pl.multiple_of(block * DH, DH), DH)]
         seg_halo = seg_ref[b : b + 1, pl.ds(pl.multiple_of(before * DH, DH), DH)]
@@ -211,16 +228,6 @@
     pick_ref[0] = jnp.where(in_own, 0.0, 1.0).astype(jnp.bfloat16)
     pick_ref[1] = jnp.where(in_own, 1.0, 0.0).astype(jnp.bfloat16)
 
-    pl.semaphore_wait(barrier, sum(exists.astype(jnp.int32) for exists, _ in neighbours))
-
-    @pl.when(has_right)
-    def _():
-        def send_halo(item):
-            for copy in halo_copies(item):
-                copy.start()
-
-        loop(items, send_halo)
-
     def merge(both):
         count = both.shape[1] // DH
         keep = jnp.concatenate([in_own] * count, axis=1)
@@ -243,18 +250,31 @@
 
         key = kv_buf[item, 0].reshape(2 * DH, DH)
         bias = bias_ref[item // kv_heads]
-        for part in range(per_item):
-            cols = slice(part * wide, (part + 1) * wide)
-            query = stack_heads(x_buf[item, :, cols])
-            score = merge(dot(key, query, NT)) + jnp.concatenate([bias] * CHUNK, axis=1)
-            top = jnp.max(score, axis=0, keepdims=True)
-            weight = jnp.exp2((score - top) * (scale * LOG2E))
-            total = jnp.sum(weight, axis=0, keepdims=True)
-            prob_buf[item, :, cols] = weight * (1.0 / total)
+        query = stack_heads(x_buf[item])
+        score = merge(dot(key, query, NT)) + jnp.concatenate([bias] * group, axis=1)
+        top = jnp.max(score, axis=0, keepdims=True)
+        weight = jnp.exp2((score - top) * (scale * LOG2E))
+        total = jnp.sum(weight, axis=0, keepdims=True)
+        prob_buf[item] = weight * (1.0 / total)
 
     @pl.when(jnp.logical_not(last))
     def _():
         loop(items, probabilities)
+
+    def key_value_grads(item):
+        query = stack_heads(x_buf[item])
+        grad = jnp.concatenate(
+            [stack_heads(g_in[item * per_item + part]) for part in range(per_item)], axis=0
+        )
+        key_grad = dot(ds_buf[item], query, NN) * scale
+        value_grad = dot(spread(prob_buf[item].astype(jnp.bfloat16)), grad, NN)
+        for i, total in enumerate((key_grad, value_grad)):
+            part_send[item, i] = total[:DH].astype(jnp.bfloat16)
+            part_own[item, i] = total[DH:]
+
+        @pl.when(has_left)
+        def _():
+            part_copy(item).start()
 
     def backward(item):
         @pl.when(last)
@@ -263,18 +283,17 @@
 
         key = kv_buf[item, 0].reshape(2 * DH, DH)
         value = kv_buf[item, 1].reshape(2 * DH, DH)
-        key_grad = value_grad = None
         for part in range(per_item):
             chunk = item * per_item + part
             pltpu.make_async_copy(g_in.at[chunk], g_in.at[chunk], g_recv.at[chunk]).wait()
             cols = slice(part * wide, (part + 1) * wide)
-            query = stack_heads(x_buf[item, :, cols])
             grad = stack_heads(g_in[chunk])
             prob = prob_buf[item, :, cols]
             prob_low = prob.astype(jnp.bfloat16)
             grad_prob = merge(dot(value, grad, NT))
             delta = jnp.sum(prob_low.astype(jnp.float32) * grad_prob, axis=0, keepdims=True)
             grad_score = spread((prob * (grad_prob - delta)).astype(jnp.bfloat16))
+            ds_buf[item, :, cols] = grad_score
             query_grad = dot(grad_score, key, TN) * scale
             grad_next = (grad.astype(jnp.float32) + query_grad).astype(jnp.bfloat16)
             for i in range(CHUNK):
@@ -285,19 +304,16 @@
                 grad_copy(chunk).start()
 
             out_copy(chunk).start()
-            key_part = dot(grad_score, query, NN)
-            value_part = dot(spread(prob_low), grad, NN)
-            key_grad = key_part if part == 0 else key_grad + key_part
-            value_grad = value_part if part == 0 else value_grad + value_part
-        for i, total in enumerate((key_grad * scale, value_grad)):
-            part_send[item, i] = total[:DH].astype(jnp.bfloat16)
-            part_own[item, i] = total[DH:]
-
-        @pl.when(has_left)
-        def _():
-            part_copy(item).start()
+
+        @pl.when(jnp.logical_not(has_next))
+        def _():
+            key_value_grads(item)
 
     loop(items, backward)
+
+    @pl.when(has_next)
+    def _():
+        loop(items, key_value_grads)
 
     def finish(item):
         @pl.when(has_right)
@@ -351,12 +367,13 @@
             jax.ShapeDtypeStruct(keys.shape, low),
             jax.ShapeDtypeStruct(values.shape, low),
         ),
-        in_specs=[anywhere] * 4 + [pl.BlockSpec(memory_space=pltpu.VMEM)],
+        in_specs=[anywhere] * 5,
         out_specs=(anywhere,) * 3,
         scratch_shapes=[
             pltpu.VMEM((items, rows, group * DH), low),
             pltpu.VMEM((items, 2, 2, rows, DH), low),
             pltpu.VMEM((items, rows, group * DH), full),
+            pltpu.VMEM((items, 2 * rows, group * DH), low),
             pltpu.VMEM((chunks, rows, CHUNK * DH), low),
             pltpu.VMEM((chunks, rows, CHUNK * DH), low),
             pltpu.VMEM((items, 2, rows, DH), full),
@@ -365,6 +382,8 @@
             pltpu.VMEM((items, 2, rows, DH), low),
             pltpu.VMEM((micro, DH, DH), full),
             pltpu.VMEM((2, DH, DH), low),
+            pltpu.VMEM(segments.shape, jnp.int32),
+            dma(()),
             dma((items,)),
             dma((items, 2)),
             dma((items, 2)),
@@ -377,7 +396,7 @@
             dma((items, 2)),
         ],
         compiler_params=pltpu.CompilerParams(
-            collective_id=0, has_side_effects=True, vmem_limit_bytes=40 * 1024 * 1024
+            collective_id=0, has_side_effects=True, vmem_limit_bytes=60 * 1024 * 1024
         ),
         cost_estimate=pl.CostEstimate(
             flops=10 * items * group * rows * 2 * rows * DH,

time: 51.8 us -> 49.7 us (0.959)
  local copies, waits for them, and re-layouts: 7.41 us -> 4.1 us
  Pallas kernels: 43.4 us -> 44.8 us
    unnamed x13 -> x7, local copies, waits for them, and re-layouts: 7.41 us -> 4.1 us
    pallas_call x1, Pallas kernels: 43.4 us -> 44.8 us  [per_device(): pl.pallas_call(functools.partial(kernel, sections, seq_size, kv_heads, gr...]
where the time goes in v2:
time: 49.7 us; the launch traced here: 49.5 us
  Pallas kernels  44.8 us (90%)
  local copies, waits for them, and re-layouts  4.1 us (8%)
  between operations  0.65 us (1%)
    pallas_call x1, Pallas kernels, per_device(): pl.pallas_call(functools.partial(kernel, sections, seq_size, kv_heads, gr...  44.8 us
    unnamed x7, local copies, waits for them, and re-layouts  4.1 us

profile of v2, /device:TPU:1, one launch (start us, length us, event | category | flops | bytes accessed | tf_op | source)
XLA Modules:
  0.0 49.5 jit_solution(17897626046604569681)
XLA Ops:
  0.6 44.8 %shard_map.76 = (bf16[1,2,128,2048]{3,2,1,0:T(8,128)(2,1)}, bf16[1,2,128,512]{3,2,1,0:T(8,128)(2,1)}, bf16[1,2,128,512]{3,2,1,0:T(8,128)(2,1)}) custom-call(bf16[1,2,128,2048]{3,2,1,0:T(8,128)(2,1)} %q_hbm.1, bf16[1,2,128,512]{3,2,1,0:T(8,128)(2,1)} %k_hbm.1, bf16[1,2,128,512]{3,2,1,0:T(8,128)(2,1)} %v_hbm.1, bf16[2,128,2048]{2,1,0:T(8,128)(2,1)} %g_hbm.1, ...), custom_call_target="tpu_custom_call" | custom-call | flops 1342177280 | bytes 6291456 | tf_op jit(solution)/shard_map/pallas_call | solution.py:363
  45.4 0.0 copy-start.1
  45.4 2.3 %copy.11 = bf16[1,2,128,2048]{3,2,1,0:T(8,128)(2,1)} copy(bf16[1,2,128,2048]{3,2,1,0:T(8,128)(2,1)} %get-tuple-element.6) | data formatting | bytes 2097152
  47.8 0.0 copy-done.1
  47.8 0.0 copy-start
  47.8 0.7 %copy.12 = bf16[1,2,128,512]{3,2,1,0:T(8,128)(2,1)} copy(bf16[1,2,128,512]{3,2,1,0:T(8,128)(2,1)S(1)} %copy-done.1) | data formatting | bytes 524288
  48.5 0.3 copy-done
  48.8 0.7 %copy.13 = bf16[1,2,128,512]{3,2,1,0:T(8,128)(2,1)} copy(bf16[1,2,128,512]{3,2,1,0:T(8,128)(2,1)S(1)} %copy-done) | data formatting | bytes 524288
Async XLA Ops:
  45.4 2.4 %copy-start.1 = (bf16[1,2,128,512]{3,2,1,0:T(8,128)(2,1)S(1)}, bf16[1,2,128,512]{3,2,1,0:T(8,128)(2,1)}, u32[]{:S(2)}) copy-start(bf16[1,2,128,512]{3,2,1,0:T(8,128)(2,1)} %get-tuple-element.7) | copy-start | bytes 786436
  47.8 1.0 %copy-start = (bf16[1,2,128,512]{3,2,1,0:T(8,128)(2,1)S(1)}, bf16[1,2,128,512]{3,2,1,0:T(8,128)(2,1)}, u32[]{:S(2)}) copy-start(bf16[1,2,128,512]{3,2,1,0:T(8,128)(2,1)} %get-tuple-element.8) | copy-start | bytes 786436

commit v3 on v2

--- a/solution.py
+++ b/solution.py
@@ -10,7 +10,7 @@
 DH = 128
 LOG2E = 1.4426950408889634
 MESH = pl.DeviceIdType.MESH
-CHUNK = 1
+CHUNK = 2
 
 NT = (((1,), (1,)), ((), ()))
 TN = (((0,), (0,)), ((), ()))
@@ -239,7 +239,7 @@
             [jnp.concatenate([pick_ref[i]] * count, axis=1) * packed for i in range(2)], axis=0
         )
 
-    def probabilities(item):
+    def arrive(item):
         for copy in own_copies(item):
             copy.wait()
 
@@ -248,39 +248,43 @@
             for copy in halo_copies(item):
                 copy.wait_recv()
 
+    def probabilities(item, cols):
         key = kv_buf[item, 0].reshape(2 * DH, DH)
-        bias = bias_ref[item // kv_heads]
-        query = stack_heads(x_buf[item])
-        score = merge(dot(key, query, NT)) + jnp.concatenate([bias] * group, axis=1)
+        query = stack_heads(x_buf[item, :, cols])
+        bias = jnp.concatenate([bias_ref[item // kv_heads]] * (query.shape[0] // DH), axis=1)
+        score = merge(dot(key, query, NT)) + bias
         top = jnp.max(score, axis=0, keepdims=True)
         weight = jnp.exp2((score - top) * (scale * LOG2E))
         total = jnp.sum(weight, axis=0, keepdims=True)
-        prob_buf[item] = weight * (1.0 / total)
-
-    @pl.when(jnp.logical_not(last))
-    def _():
-        loop(items, probabilities)
-
-    def key_value_grads(item):
+        prob_buf[item, :, cols] = weight * (1.0 / total)
+
+    whole = slice(0, group * DH)
+
+    def store_part(item, i, total):
+        part_send[item, i] = total[:DH].astype(jnp.bfloat16)
+        part_own[item, i] = total[DH:]
+
+    def key_grad(item):
         query = stack_heads(x_buf[item])
+        store_part(item, 0, dot(ds_buf[item], query, NN) * scale)
+
+    def value_grad(item):
         grad = jnp.concatenate(
             [stack_heads(g_in[item * per_item + part]) for part in range(per_item)], axis=0
         )
-        key_grad = dot(ds_buf[item], query, NN) * scale
-        value_grad = dot(spread(prob_buf[item].astype(jnp.bfloat16)), grad, NN)
-        for i, total in enumerate((key_grad, value_grad)):
-            part_send[item, i] = total[:DH].astype(jnp.bfloat16)
-            part_own[item, i] = total[DH:]
-
+        store_part(item, 1, dot(spread(prob_buf[item].astype(jnp.bfloat16)), grad, NN))
+
+    def send_part(item):
         @pl.when(has_left)
         def _():
             part_copy(item).start()
 
-    def backward(item):
-        @pl.when(last)
-        def _():
-            probabilities(item)
-
+    def both_grads(item):
+        key_grad(item)
+        value_grad(item)
+        send_part(item)
+
+    def backward(item, beside):
         key = kv_buf[item, 0].reshape(2 * DH, DH)
         value = kv_buf[item, 1].reshape(2 * DH, DH)
         for part in range(per_item):
@@ -293,11 +297,12 @@
             grad_prob = merge(dot(value, grad, NT))
             delta = jnp.sum(prob_low.astype(jnp.float32) * grad_prob, axis=0, keepdims=True)
             grad_score = spread((prob * (grad_prob - delta)).astype(jnp.bfloat16))
-            ds_buf[item, :, cols] = grad_score
             query_grad = dot(grad_score, key, TN) * scale
             grad_next = (grad.astype(jnp.float32) + query_grad).astype(jnp.bfloat16)
             for i in range(CHUNK):
                 g_out[chunk, :, i * DH : (i + 1) * DH] = grad_next[i * DH : (i + 1) * DH]
+            beside(part)
+            ds_buf[item, :, cols] = grad_score
 
             @pl.when(has_next)
             def _():
@@ -305,15 +310,47 @@
 
             out_copy(chunk).start()
 
-        @pl.when(jnp.logical_not(has_next))
-        def _():
-            key_value_grads(item)
-
-    loop(items, backward)
-
-    @pl.when(has_next)
-    def _():
-        loop(items, key_value_grads)
+    def nothing(part):
+        pass
+
+    @pl.when(last)
+    def _():
+        arrive(0)
+        probabilities(0, whole)
+
+        def one(item):
+            arrive(item + 1)
+
+            def ahead(part):
+                probabilities(item + 1, slice(part * wide, (part + 1) * wide))
+
+            backward(item, ahead)
+
+        loop(items - 1, one)
+        backward(items - 1, nothing)
+        loop(items, both_grads)
+
+    @pl.when(jnp.logical_not(last))
+    def _():
+        def prepare(item):
+            arrive(item)
+            probabilities(item, whole)
+
+        loop(items, prepare)
+        backward(0, nothing)
+
+        def one(i):
+            def behind(part):
+                if part == 0:
+                    key_grad(i)
+                if part == per_item - 1:
+                    value_grad(i)
+
+            backward(i + 1, behind)
+            send_part(i)
+
+        loop(items - 1, one)
+        both_grads(items - 1)
 
     def finish(item):
         @pl.when(has_right)
@@ -348,6 +385,20 @@
             part_copy(item).wait_send()
 
     loop(items, drain)
+
+
+def hand_over(pieces, *refs):
+    sources, results, sem = refs[:3], refs[3:6], refs[6]
+    copies = []
+    for i, (source, result) in enumerate(zip(sources, results)):
+        rows = source.shape[2] // pieces
+        for j in range(pieces):
+            at = (0, slice(None), pl.ds(j * rows, rows))
+            copies.append(pltpu.make_async_copy(source.at[at], result.at[at], sem.at[i, j]))
+    for copy in copies:
+        copy.start()
+    for copy in copies:
+        copy.wait()
 
 
 def per_device(sections, seq_size, queries, keys, values, out_grad, segments):
@@ -360,13 +411,10 @@
     anywhere = pl.BlockSpec(memory_space=pl.ANY)
     low, full = jnp.bfloat16, jnp.float32
     dma = pltpu.SemaphoreType.DMA
-    return pl.pallas_call(
+    shapes = tuple(jax.ShapeDtypeStruct(x.shape, low) for x in (queries, keys, values))
+    grads = pl.pallas_call(
         functools.partial(kernel, sections, seq_size, kv_heads, group),
-        out_shape=(
-            jax.ShapeDtypeStruct(queries.shape, low),
-            jax.ShapeDtypeStruct(keys.shape, low),
-            jax.ShapeDtypeStruct(values.shape, low),
-        ),
+        out_shape=shapes,
         in_specs=[anywhere] * 5,
         out_specs=(anywhere,) * 3,
         scratch_shapes=[
@@ -404,6 +452,15 @@
             transcendentals=items * group * rows * rows,
         ),
     )(queries, keys, values, out_grad, segments)
+    pieces = 4
+    return pl.pallas_call(
+        functools.partial(hand_over, pieces),
+        out_shape=shapes,
+        in_specs=[anywhere] * 3,
+        out_specs=(anywhere,) * 3,
+        scratch_shapes=[dma((3, pieces))],
+        compiler_params=pltpu.CompilerParams(vmem_limit_bytes=60 * 1024 * 1024),
+    )(*grads)
 
 
 def solution(mesh):

time: 49.7 us -> 94.1 us (1.89)
  Pallas kernels: 44.8 us -> 93.3 us
  local copies, waits for them, and re-layouts: 4.1 us -> 0 us
    pallas_call x0 -> x1, Pallas kernels: none -> 48.9 us  [per_device(): pl.pallas_call(functools.partial(hand_over, pieces), out_shape=shapes, in...]
    unnamed x7 -> x0, local copies, waits for them, and re-layouts: 4.1 us -> none
where the time goes in v3:
time: 94.1 us; the launch traced here: 93.9 us
  Pallas kernels  93.3 us (99%)
    pallas_call x1, Pallas kernels, per_device(): pl.pallas_call(functools.partial(hand_over, pieces), out_shape=shapes, in...  48.9 us
    pallas_call x1, Pallas kernels, per_device(): pl.pallas_call(functools.partial(kernel, sections, seq_size, kv_heads, gr...  44.4 us

profile of v3, /device:TPU:1, one launch (start us, length us, event | category | flops | bytes accessed | tf_op | source)
XLA Modules:
  0.0 93.9 jit_solution(6796588055793592181)
XLA Ops:
  0.6 44.4 %shard_map.76 = (bf16[1,2,128,2048]{3,2,1,0:T(8,128)(2,1)}, bf16[1,2,128,512]{3,2,1,0:T(8,128)(2,1)}, bf16[1,2,128,512]{3,2,1,0:T(8,128)(2,1)}) custom-call(bf16[1,2,128,2048]{3,2,1,0:T(8,128)(2,1)} %q_hbm.1, bf16[1,2,128,512]{3,2,1,0:T(8,128)(2,1)} %k_hbm.1, bf16[1,2,128,512]{3,2,1,0:T(8,128)(2,1)} %v_hbm.1, bf16[2,128,2048]{2,1,0:T(8,128)(2,1)} %g_hbm.1, ...), custom_call_target="tpu_custom_call" | custom-call | flops 1342177280 | bytes 6291456 | tf_op jit(solution)/shard_map/pallas_call | solution.py:415
  45.0 48.9 %shard_map.77 = (bf16[1,2,128,2048]{3,2,1,0:T(8,128)(2,1)}, bf16[1,2,128,512]{3,2,1,0:T(8,128)(2,1)}, bf16[1,2,128,512]{3,2,1,0:T(8,128)(2,1)}) custom-call(bf16[1,2,128,2048]{3,2,1,0:T(8,128)(2,1)} %get-tuple-element.6.refs_0_, bf16[1,2,128,512]{3,2,1,0:T(8,128)(2,1)} %get-tuple-element.7.refs_1_, bf16[1,2,128,512]{3,2,1,0:T(8,128)(2,1)} %get-tuple-element.8.refs_2_), custom_call_target="tpu_custom_call" | custom-call | tf_op jit(solution)/shard_map/pallas_call | solution.py:456

commit v4 on v3

v4 whole, which is shorter than its diff:
```python
import functools

import jax
import jax.numpy as jnp
from jax import lax
from jax.experimental import pallas as pl
from jax.experimental.pallas import tpu as pltpu
from jax.sharding import PartitionSpec as P

DH = 128
LOG2E = 1.4426950408889634
MESH = pl.DeviceIdType.MESH

NT = (((1,), (1,)), ((), ()))
TN = (((0,), (0,)), ((), ()))
NN = (((1,), (0,)), ((), ()))


def dot(left, right, dims):
    return lax.dot_general(left, right, dims, preferred_element_type=jnp.float32)


def stack_heads(rows):
    count = rows.shape[1] // DH
    return jnp.concatenate([rows[:, i * DH : (i + 1) * DH] for i in range(count)], axis=0)


def loop(start, stop, body):
    def step(i, carry):
        body(i)
        return carry

    lax.fori_loop(start, stop, step, 0)


def kernel(
    sections,
    seq_size,
    kv_heads,
    group,
    q_hbm,
    k_hbm,
    v_hbm,
    g_hbm,
    seg_hbm,
    qg_hbm,
    kg_hbm,
    vg_hbm,
    x_buf,
    kv_buf,
    top_buf,
    prob_buf,
    ds_buf,
    g_in,
    g_out,
    qg_buf,
    part_own,
    part_send,
    part_recv,
    kv_out,
    bias_ref,
    pick_ref,
    seg_ref,
    seg_sem,
    x_sem,
    top_sem,
    own_sem,
    halo_send,
    halo_recv,
    g_send,
    g_recv,
    part_send_sem,
    part_recv_sem,
    qg_sem,
    kvg_sem,
):
    section = lax.axis_index("pipe")
    block = lax.axis_index("seq")
    micro = q_hbm.shape[1]
    items = micro * kv_heads
    scale = DH**-0.5
    last = section == sections - 1
    has_next = section > 0
    has_left = block > 0
    has_right = block < seq_size - 1
    edge = tuple((i, 1) for i in range(group))
    inner = tuple((i, 2) for i in range(0, group, 2)) if group % 2 == 0 else edge

    def place(item):
        head = lax.rem(item, kv_heads)
        return (
            item // kv_heads,
            pl.multiple_of(head * DH, DH),
            pl.multiple_of(head * group * DH, DH),
        )

    seg_copy = pltpu.make_async_copy(seg_hbm, seg_ref, seg_sem)

    def x_copy(b):
        return pltpu.make_async_copy(q_hbm.at[0, b], x_buf.at[b], x_sem.at[b])

    def top_copy(b):
        return pltpu.make_async_copy(g_hbm.at[b], top_buf.at[b], top_sem.at[b])

    def own_copies(b):
        return tuple(
            pltpu.make_async_copy(ref.at[0, b], kv_buf.at[i, b, 1], own_sem.at[i, b])
            for i, ref in enumerate((k_hbm, v_hbm))
        )

    def halo_copies(b, stage):
        width = kv_heads * DH
        cols = {0: pl.ds(0, DH), 1: pl.ds(DH, width - DH), 2: pl.ds(0, width)}[stage]
        at = b + 1 if stage == 2 else stage
        return tuple(
            pltpu.make_async_remote_copy(
                src_ref=ref.at[0, b, :, cols],
                dst_ref=kv_buf.at[i, b, 0, :, cols],
                send_sem=halo_send.at[i, at],
                recv_sem=halo_recv.at[i, at],
                device_id=(section, block + 1),
                device_id_type=MESH,
            )
            for i, ref in enumerate((k_hbm, v_hbm))
        )

    all_halos = [(0, 0)] + ([(0, 1)] if kv_heads > 1 else []) + [(b, 2) for b in range(1, micro)]

    def grad_copy(item, head, count):
        return pltpu.make_async_remote_copy(
            src_ref=g_out.at[item, pl.ds(head, count)],
            dst_ref=g_in.at[item, pl.ds(head, count)],
            send_sem=g_send,
            recv_sem=g_recv.at[item, head],
            device_id=(section - 1, block),
            device_id_type=MESH,
        )

    def part_copy(item):
        return pltpu.make_async_remote_copy(
            src_ref=part_send.at[item],
            dst_ref=part_recv.at[item],
            send_sem=part_send_sem,
            recv_sem=part_recv_sem,
            device_id=(section, block - 1),
            device_id_type=MESH,
        )

    barrier = pltpu.get_barrier_semaphore()
    neighbours = (
        (has_right, (section, block + 1)),
        (has_left, (section, block - 1)),
        (has_next, (section - 1, block)),
        (section < sections - 1, (section + 1, block)),
    )
    for exists, device in neighbours:

        @pl.when(exists)
        def _(device=device):
            pl.semaphore_signal(barrier, inc=1, device_id=device, device_id_type=MESH)

    seg_copy.start()
    for b in range(micro):
        for copy in own_copies(b):
            copy.start()
        x_copy(b).start()

        @pl.when(last)
        def _(b=b):
            top_copy(b).start()

    pl.semaphore_wait(barrier, sum(exists.astype(jnp.int32) for exists, _ in neighbours))

    @pl.when(has_right)
    def _():
        for b, stage in all_halos:
            for copy in halo_copies(b, stage):
                copy.start()

    @pl.when(jnp.logical_not(has_left))
    def _():
        for i in range(2):
            for b in range(micro):
                kv_buf[i, b, 0] = jnp.zeros(kv_buf.shape[3:], jnp.bfloat16)

    @pl.when(jnp.logical_not(has_right))
    def _():
        def clear(item):
            part_recv[item] = jnp.zeros(part_recv.shape[1:], jnp.bfloat16)

        loop(0, items, clear)

    key_at = lax.broadcasted_iota(jnp.int32, (DH, DH), 0)
    query_at = lax.broadcasted_iota(jnp.int32, (DH, DH), 1)
    in_own = key_at <= query_at
    before = jnp.maximum(block - 1, 0)
    seg_copy.wait()
    for b in range(micro):
        seg_query = seg_ref[b : b + 1, pl.ds(pl.multiple_of(block * DH, DH), DH)]
        seg_halo = seg_ref[b : b + 1, pl.ds(pl.multiple_of(before * DH, DH), DH)]
        seg_query = jnp.broadcast_to(seg_query.astype(jnp.float32), (DH, DH))
        seg_halo = jnp.broadcast_to(seg_halo.astype(jnp.float32), (DH, DH))
        seg_halo = jnp.where(has_left, seg_halo, -1.0)
        seg_key = jnp.where(in_own, seg_query.T, seg_halo.T)
        bias_ref[b] = jnp.where(seg_key == seg_query, 0.0, -1e30)
    pick_ref[0] = jnp.where(in_own, 0.0, 1.0).astype(jnp.bfloat16)
    pick_ref[1] = jnp.where(in_own, 1.0, 0.0).astype(jnp.bfloat16)

    def merge(both):
        count = both.shape[1] // DH
        keep = jnp.concatenate([in_own] * count, axis=1)
        return jnp.where(keep, both[DH:], both[:DH])

    def spread(packed):
        count = packed.shape[1] // DH
        return jnp.concatenate(
            [jnp.concatenate([pick_ref[i]] * count, axis=1) * packed for i in range(2)], axis=0
        )

    def rows_of(i, item):
        b, col, _ = place(item)
        return kv_buf[i, b, :, :, pl.ds(col, DH)].reshape(2 * DH, DH)

    def heads_of(ref, item, head, count):
        b, _, col = place(item)
        at = pl.multiple_of(col + head * DH, DH)
        return stack_heads(ref[b, :, pl.ds(at, count * DH)])

    def wait_halo(b, stage):
        @pl.when(has_left)
        def _():
            for copy in halo_copies(b, stage):
                copy.wait_recv()

    def wait_batch(b):
        for copy in own_copies(b):
            copy.wait()
        x_copy(b).wait()

        @pl.when(last)
        def _():
            top_copy(b).wait()

    def wait_first():
        wait_batch(0)
        wait_halo(0, 0)

    def wait_second():
        if kv_heads > 1:
            wait_halo(0, 1)

    def wait_later(b):
        wait_batch(b)
        wait_halo(b, 2)

    def probabilities(item, head, count):
        query = heads_of(x_buf, item, head, count)
        bias = jnp.concatenate([bias_ref[item // kv_heads]] * count, axis=1)
        score = merge(dot(rows_of(0, item), query, NT)) + bias
        top = jnp.max(score, axis=0, keepdims=True)
        weight = jnp.exp2((score - top) * (scale * LOG2E))
        total = jnp.sum(weight, axis=0, keepdims=True)
        prob_buf[item, :, head * DH : (head + count) * DH] = weight * (1.0 / total)

    def store_part(item, i, total):
        part_send[item, i] = total[:DH].astype(jnp.bfloat16)
        part_own[item, i] = total[DH:]

    def key_grad(item):
        query = heads_of(x_buf, item, 0, group)
        store_part(item, 0, dot(ds_buf[item], query, NN) * scale)

    def top_grad(item, head, count):
        return heads_of(top_buf, item, head, count)

    def sent_grad(item, head, count):
        return g_in[item, head : head + count].reshape(count * DH, DH)

    def value_grad(item, grad_of):
        grad = grad_of(item, 0, group)
        store_part(item, 1, dot(spread(prob_buf[item].astype(jnp.bfloat16)), grad, NN))

    def send_part(item):
        @pl.when(has_left)
        def _():
            part_copy(item).start()

    def both_grads(item, grad_of):
        key_grad(item)
        value_grad(item, grad_of)
        send_part(item)

    def backward(item, messages, grad_of, beside):
        b, _, wide_col = place(item)
        for head, count in messages:
            if grad_of is sent_grad:
                grad_copy(item, head, count).wait_recv()
            beside(head, count, True)
            cols = slice(head * DH, (head + count) * DH)
            key, value = rows_of(0, item), rows_of(1, item)
            grad = grad_of(item, head, count)
            prob = prob_buf[item, :, cols]
            prob_low = prob.astype(jnp.bfloat16)
            grad_prob = merge(dot(value, grad, NT))
            delta = jnp.sum(prob_low.astype(jnp.float32) * grad_prob, axis=0, keepdims=True)
            grad_score = spread((prob * (grad_prob - delta)).astype(jnp.bfloat16))
            query_grad = dot(grad_score, key, TN) * scale
            grad_next = (grad.astype(jnp.float32) + query_grad).astype(jnp.bfloat16)
            g_out[item, head : head + count] = grad_next.reshape(count, DH, DH)
            beside(head, count, False)
            ds_buf[item, :, cols] = grad_score

            @pl.when(has_next)
            def _():
                grad_copy(item, head, count).start()

            for i in range(count):
                at = pl.multiple_of(wide_col + (head + i) * DH, DH)
                qg_buf[b, :, pl.ds(at, DH)] = grad_next[i * DH : (i + 1) * DH]
        at = pl.ds(wide_col, group * DH)
        pltpu.make_async_copy(qg_buf.at[b, :, at], qg_hbm.at[0, b, :, at], qg_sem).start()

    def nothing(head, count, first):
        pass

    @pl.when(last)
    def _():
        wait_first()

        def at_once(head, count, first):
            if first:
                probabilities(0, head, count)

        backward(0, edge, top_grad, at_once)
        wait_second()
        probabilities(1, 0, group)

        def one(item):
            @pl.when(lax.rem(item + 1, kv_heads) == 0)
            def _():
                wait_later((item + 1) // kv_heads)

            def ahead(head, count, first):
                if not first:
                    probabilities(item + 1, head, count)

            backward(item, inner, top_grad, ahead)

        loop(1, items - 1, one)
        backward(items - 1, edge, top_grad, nothing)
        loop(0, items, lambda item: both_grads(item, top_grad))

    @pl.when(jnp.logical_not(last))
    def _():
        wait_first()
        wait_second()
        loop(0, kv_heads, lambda item: probabilities(item, 0, group))
        for b in range(1, micro):
            wait_later(b)
        loop(kv_heads, items, lambda item: probabilities(item, 0, group))
        backward(0, edge, sent_grad, nothing)

        def behind_of(i, half):
            def behind(head, count, first):
                if not first and head == 0:
                    key_grad(i)
                if not first and head == half:
                    value_grad(i, sent_grad)

            return behind

        def one(item):
            backward(item, inner, sent_grad, behind_of(item - 1, inner[-1][0]))
            send_part(item - 1)

        loop(1, items - 1, one)
        backward(items - 1, edge, sent_grad, behind_of(items - 2, 1))
        send_part(items - 2)
        both_grads(items - 1, sent_grad)

    @pl.when(has_right)
    def _():
        pltpu.make_async_copy(part_recv, part_recv, part_recv_sem).wait()

    def finish(item):
        b, col, _ = place(item)
        for i in range(2):
            total = part_own[item, i] + part_recv[item, i].astype(jnp.float32)
            kv_out[i, b, :, pl.ds(col, DH)] = total.astype(jnp.bfloat16)

    loop(0, items, finish)
    results = tuple(
        pltpu.make_async_copy(kv_out.at[i], ref.at[0], kvg_sem.at[i])
        for i, ref in enumerate((kg_hbm, vg_hbm))
    )
    for copy in results:
        copy.start()

    @pl.when(has_next)
    def _():
        pltpu.make_async_copy(g_out, g_out, g_send).wait()

    @pl.when(has_right)
    def _():
        for b, stage in all_halos:
            for copy in halo_copies(b, stage):
                copy.wait_send()

    @pl.when(has_left)
    def _():
        pltpu.make_async_copy(part_send, part_send, part_send_sem).wait()

    pltpu.make_async_copy(qg_buf, qg_hbm.at[0], qg_sem).wait()
    for copy in results:
        copy.wait()


def hand_over(*refs):
    count = len(refs) // 3
    sources, results, held = refs[:count], refs[count : 2 * count], refs[2 * count : 3 * count]
    sem = refs[3 * count]
    micro = sources[0].shape[1]
    takes, gives = [], []
    for i in range(count):
        for b in range(micro):
            at = (0, b)
            takes.append(pltpu.make_async_copy(sources[i].at[at], held[i].at[at], sem.at[0, i, b]))
            gives.append(pltpu.make_async_copy(held[i].at[at], results[i].at[at], sem.at[1, i, b]))
    for take in takes:
        take.start()
    for take, give in zip(takes, gives):
        take.wait()
        give.start()
    for give in gives:
        give.wait()


def per_device(sections, seq_size, queries, keys, values, out_grad, segments):
    micro, rows, query_width = queries.shape[1:]
    key_width = keys.shape[3]
    kv_heads = key_width // DH
    group = query_width // key_width
    items = micro * kv_heads
    anywhere = pl.BlockSpec(memory_space=pl.ANY)
    low, full = jnp.bfloat16, jnp.float32
    dma = pltpu.SemaphoreType.DMA
    shapes = tuple(jax.ShapeDtypeStruct(x.shape, low) for x in (queries, keys, values))
    grads = pl.pallas_call(
        functools.partial(kernel, sections, seq_size, kv_heads, group),
        out_shape=shapes,
        in_specs=[anywhere] * 5,
        out_specs=(anywhere,) * 3,
        scratch_shapes=[
            pltpu.VMEM((micro, rows, query_width), low),
            pltpu.VMEM((2, micro, 2, rows, key_width), low),
            pltpu.VMEM((micro, rows, query_width), low),
            pltpu.VMEM((items, rows, group * DH), full),
            pltpu.VMEM((items, 2 * rows, group * DH), low),
            pltpu.VMEM((items, group, rows, DH), low),
            pltpu.VMEM((items, group, rows, DH), low),
            pltpu.VMEM((micro, rows, query_width), low),
            pltpu.VMEM((items, 2, rows, DH), full),
            pltpu.VMEM((items, 2, rows, DH), low),
            pltpu.VMEM((items, 2, rows, DH), low),
            pltpu.VMEM((2, micro, rows, key_width), low),
            pltpu.VMEM((micro, DH, DH), full),
            pltpu.VMEM((2, DH, DH), low),
            pltpu.VMEM(segments.shape, jnp.int32),
            dma(()),
            dma((micro,)),
            dma((micro,)),
            dma((2, micro)),
            dma((2, micro + 1)),
            dma((2, micro + 1)),
            dma(()),
            dma((items, group)),
            dma(()),
            dma(()),
            dma(()),
            dma((2,)),
        ],
        compiler_params=pltpu.CompilerParams(
            collective_id=0, has_side_effects=True, vmem_limit_bytes=60 * 1024 * 1024
        ),
        cost_estimate=pl.CostEstimate(
            flops=10 * items * group * rows * 2 * rows * DH,
            bytes_accessed=6 * 1024 * 1024,
            transcendentals=items * group * rows * rows,
        ),
    )(queries, keys, values, out_grad, segments)
    return pl.pallas_call(
        hand_over,
        out_shape=shapes,
        in_specs=[anywhere] * 3,
        out_specs=(anywhere,) * 3,
        scratch_shapes=[pltpu.VMEM(x.shape, low) for x in shapes] + [dma((2, 3, micro))],
        compiler_params=pltpu.CompilerParams(vmem_limit_bytes=60 * 1024 * 1024),
    )(*grads)


def solution(mesh):
    sizes = dict(mesh.shape)
    split = P("pipe", None, "seq", None)
    return jax.shard_map(
        functools.partial(per_device, sizes["pipe"], sizes["seq"]),
        mesh=mesh,
        in_specs=(split, split, split, P(None, "seq", None), P()),
        out_specs=(split, split, split),
        check_vma=False,
    )
```

time: 94.1 us -> 48.5 us (0.52)
  Pallas kernels: 93.3 us -> 47.7 us
    pallas_call x1, Pallas kernels: 48.9 us -> 2.28 us  [per_device(): pl.pallas_call(hand_over, out_shape=shapes, in_specs=[anywhere] * 3, out_...]
    pallas_call x1, Pallas kernels: 44.4 us -> 45.4 us  [per_device(): pl.pallas_call(functools.partial(kernel, sections, seq_size, kv_heads, gr...]
where the time goes in v4:
time: 48.5 us; the launch traced here: 48.4 us
  Pallas kernels  47.7 us (98%)
  between operations  0.64 us (1%)
    pallas_call x1, Pallas kernels, per_device(): pl.pallas_call(functools.partial(kernel, sections, seq_size, kv_heads, gr...  45.4 us
    pallas_call x1, Pallas kernels, per_device(): pl.pallas_call(hand_over, out_shape=shapes, in_specs=[anywhere] * 3, out_...  2.28 us

profile of v4, /device:TPU:1, one launch (start us, length us, event | category | flops | bytes accessed | tf_op | source)
XLA Modules:
  0.0 48.4 jit_solution(8870413086814047300)
XLA Ops:
  0.6 45.4 %shard_map.76 = (bf16[1,2,128,2048]{3,2,1,0:T(8,128)(2,1)}, bf16[1,2,128,512]{3,2,1,0:T(8,128)(2,1)}, bf16[1,2,128,512]{3,2,1,0:T(8,128)(2,1)}) custom-call(bf16[1,2,128,2048]{3,2,1,0:T(8,128)(2,1)} %q_hbm.1, bf16[1,2,128,512]{3,2,1,0:T(8,128)(2,1)} %k_hbm.1, bf16[1,2,128,512]{3,2,1,0:T(8,128)(2,1)} %v_hbm.1, bf16[2,128,2048]{2,1,0:T(8,128)(2,1)} %g_hbm.1, ...), custom_call_target="tpu_custom_call" | custom-call | flops 1342177280 | bytes 6291456 | tf_op jit(solution)/shard_map/pallas_call | solution.py:448
  46.1 2.3 %shard_map.77 = (bf16[1,2,128,2048]{3,2,1,0:T(8,128)(2,1)}, bf16[1,2,128,512]{3,2,1,0:T(8,128)(2,1)}, bf16[1,2,128,512]{3,2,1,0:T(8,128)(2,1)}) custom-call(bf16[1,2,128,2048]{3,2,1,0:T(8,128)(2,1)} %get-tuple-element.6.refs_0_, bf16[1,2,128,512]{3,2,1,0:T(8,128)(2,1)} %get-tuple-element.7.refs_1_, bf16[1,2,128,512]{3,2,1,0:T(8,128)(2,1)} %get-tuple-element.8.refs_2_), custom_call_target="tpu_custom_call" | custom-call | tf_op jit(solution)/shard_map/pallas_call | solution.py:491

commit v5 on v4

--- a/solution.py
+++ b/solution.py
@@ -12,7 +12,6 @@
 MESH = pl.DeviceIdType.MESH
 
 NT = (((1,), (1,)), ((), ()))
-TN = (((0,), (0,)), ((), ()))
 NN = (((1,), (0,)), ((), ()))
 
 
@@ -49,6 +48,7 @@
     x_buf,
     kv_buf,
     top_buf,
+    key_t,
     prob_buf,
     ds_buf,
     g_in,
@@ -254,6 +254,8 @@
         wait_halo(b, 2)
 
     def probabilities(item, head, count):
+        if head == 0:
+            key_t[item] = rows_of(0, item).T
         query = heads_of(x_buf, item, head, count)
         bias = jnp.concatenate([bias_ref[item // kv_heads]] * count, axis=1)
         score = merge(dot(rows_of(0, item), query, NT)) + bias
@@ -271,14 +273,19 @@
         store_part(item, 0, dot(ds_buf[item], query, NN) * scale)
 
     def top_grad(item, head, count):
-        return heads_of(top_buf, item, head, count)
+        rows = heads_of(top_buf, item, head, count)
+        return jnp.concatenate([rows[i * DH : (i + 1) * DH].T for i in range(count)], axis=1)
 
     def sent_grad(item, head, count):
-        return g_in[item, head : head + count].reshape(count * DH, DH)
+        return jnp.concatenate([g_in[item, head + i] for i in range(count)], axis=1)
 
     def value_grad(item, grad_of):
-        grad = grad_of(item, 0, group)
-        store_part(item, 1, dot(spread(prob_buf[item].astype(jnp.bfloat16)), grad, NN))
+        prob_low = spread(prob_buf[item].astype(jnp.bfloat16))
+        if grad_of is top_grad:
+            total = dot(prob_low, heads_of(top_buf, item, 0, group), NN)
+        else:
+            total = dot(prob_low, grad_of(item, 0, group), NT)
+        store_part(item, 1, total)
 
     def send_part(item):
         @pl.when(has_left)
@@ -297,16 +304,17 @@
                 grad_copy(item, head, count).wait_recv()
             beside(head, count, True)
             cols = slice(head * DH, (head + count) * DH)
-            key, value = rows_of(0, item), rows_of(1, item)
+            value = rows_of(1, item)
             grad = grad_of(item, head, count)
             prob = prob_buf[item, :, cols]
             prob_low = prob.astype(jnp.bfloat16)
-            grad_prob = merge(dot(value, grad, NT))
+            grad_prob = merge(dot(value, grad, NN))
             delta = jnp.sum(prob_low.astype(jnp.float32) * grad_prob, axis=0, keepdims=True)
             grad_score = spread((prob * (grad_prob - delta)).astype(jnp.bfloat16))
-            query_grad = dot(grad_score, key, TN) * scale
+            query_grad = dot(key_t[item], grad_score, NN) * scale
             grad_next = (grad.astype(jnp.float32) + query_grad).astype(jnp.bfloat16)
-            g_out[item, head : head + count] = grad_next.reshape(count, DH, DH)
+            for i in range(count):
+                g_out[item, head + i] = grad_next[:, i * DH : (i + 1) * DH]
             beside(head, count, False)
             ds_buf[item, :, cols] = grad_score
 
@@ -316,7 +324,7 @@
 
             for i in range(count):
                 at = pl.multiple_of(wide_col + (head + i) * DH, DH)
-                qg_buf[b, :, pl.ds(at, DH)] = grad_next[i * DH : (i + 1) * DH]
+                qg_buf[b, :, pl.ds(at, DH)] = grad_next[:, i * DH : (i + 1) * DH].T
         at = pl.ds(wide_col, group * DH)
         pltpu.make_async_copy(qg_buf.at[b, :, at], qg_hbm.at[0, b, :, at], qg_sem).start()
 
@@ -350,7 +358,50 @@
         backward(items - 1, edge, top_grad, nothing)
         loop(0, items, lambda item: both_grads(item, top_grad))
 
-    @pl.when(jnp.logical_not(last))
+    def behind_of(i, half):
+        def behind(head, count, first):
+            if not first and head == 0:
+                key_grad(i)
+            if not first and head == half:
+                value_grad(i, sent_grad)
+
+        return behind
+
+    def one_sent(item):
+        backward(item, inner, sent_grad, behind_of(item - 1, inner[-1][0]))
+        send_part(item - 1)
+
+    def last_sent():
+        backward(items - 1, edge, sent_grad, behind_of(items - 2, 1))
+        send_part(items - 2)
+        both_grads(items - 1, sent_grad)
+
+    @pl.when(section == sections - 2)
+    def _():
+        lead = kv_heads - 1
+        wait_first()
+        wait_second()
+        loop(0, kv_heads, lambda item: probabilities(item, 0, group))
+        backward(0, edge, sent_grad, nothing)
+        for b in range(1, micro):
+            wait_later(b)
+
+        def both(item):
+            behind = behind_of(item - 1, inner[-1][0])
+
+            def beside(head, count, first):
+                behind(head, count, first)
+                if not first:
+                    probabilities(item + lead, head, count)
+
+            backward(item, inner, sent_grad, beside)
+            send_part(item - 1)
+
+        loop(1, items - lead, both)
+        loop(items - lead, items - 1, one_sent)
+        last_sent()
+
+    @pl.when(section < sections - 2)
     def _():
         wait_first()
         wait_second()
@@ -359,24 +410,8 @@
             wait_later(b)
         loop(kv_heads, items, lambda item: probabilities(item, 0, group))
         backward(0, edge, sent_grad, nothing)
-
-        def behind_of(i, half):
-            def behind(head, count, first):
-                if not first and head == 0:
-                    key_grad(i)
-                if not first and head == half:
-                    value_grad(i, sent_grad)
-
-            return behind
-
-        def one(item):
-            backward(item, inner, sent_grad, behind_of(item - 1, inner[-1][0]))
-            send_part(item - 1)
-
-        loop(1, items - 1, one)
-        backward(items - 1, edge, sent_grad, behind_of(items - 2, 1))
-        send_part(items - 2)
-        both_grads(items - 1, sent_grad)
+        loop(1, items - 1, one_sent)
+        last_sent()
 
     @pl.when(has_right)
     def _():
@@ -454,6 +489,7 @@
             pltpu.VMEM((micro, rows, query_width), low),
             pltpu.VMEM((2, micro, 2, rows, key_width), low),
             pltpu.VMEM((micro, rows, query_width), low),
+            pltpu.VMEM((items, DH, 2 * rows), low),
             pltpu.VMEM((items, rows, group * DH), full),
             pltpu.VMEM((items, 2 * rows, group * DH), low),
             pltpu.VMEM((items, group, rows, DH), low),

time: 48.5 us -> 47.9 us (0.988)
  Pallas kernels: 47.7 us -> 47.2 us
    pallas_call x1, Pallas kernels: 45.4 us -> 44.9 us  [per_device(): pl.pallas_call(functools.partial(kernel, sections, seq_size, kv_heads, gr...]
where the time goes in v5:
time: 47.9 us; the launch traced here: 47.8 us
  Pallas kernels  47.2 us (99%)
  between operations  0.64 us (1%)
    pallas_call x1, Pallas kernels, per_device(): pl.pallas_call(functools.partial(kernel, sections, seq_size, kv_heads, gr...  44.9 us
    pallas_call x1, Pallas kernels, per_device(): pl.pallas_call(hand_over, out_shape=shapes, in_specs=[anywhere] * 3, out_...  2.28 us

profile of v5, /device:TPU:1, one launch (start us, length us, event | category | flops | bytes accessed | tf_op | source)
XLA Modules:
  0.0 47.8 jit_solution(3568966751872702242)
XLA Ops:
  0.6 44.9 %shard_map.76 = (bf16[1,2,128,2048]{3,2,1,0:T(8,128)(2,1)}, bf16[1,2,128,512]{3,2,1,0:T(8,128)(2,1)}, bf16[1,2,128,512]{3,2,1,0:T(8,128)(2,1)}) custom-call(bf16[1,2,128,2048]{3,2,1,0:T(8,128)(2,1)} %q_hbm.1, bf16[1,2,128,512]{3,2,1,0:T(8,128)(2,1)} %k_hbm.1, bf16[1,2,128,512]{3,2,1,0:T(8,128)(2,1)} %v_hbm.1, bf16[2,128,2048]{2,1,0:T(8,128)(2,1)} %g_hbm.1, ...), custom_call_target="tpu_custom_call" | custom-call | flops 1342177280 | bytes 6291456 | tf_op jit(solution)/shard_map/pallas_call | solution.py:483
  45.5 2.3 %shard_map.77 = (bf16[1,2,128,2048]{3,2,1,0:T(8,128)(2,1)}, bf16[1,2,128,512]{3,2,1,0:T(8,128)(2,1)}, bf16[1,2,128,512]{3,2,1,0:T(8,128)(2,1)}) custom-call(bf16[1,2,128,2048]{3,2,1,0:T(8,128)(2,1)} %get-tuple-element.6.refs_0_, bf16[1,2,128,512]{3,2,1,0:T(8,128)(2,1)} %get-tuple-element.7.refs_1_, bf16[1,2,128,512]{3,2,1,0:T(8,128)(2,1)} %get-tuple-element.8.refs_2_), custom_call_target="tpu_custom_call" | custom-call | tf_op jit(solution)/shard_map/pallas_call | solution.py:527

commit v6 on v5

--- a/solution.py
+++ b/solution.py
@@ -126,10 +126,10 @@
 
     all_halos = [(0, 0)] + ([(0, 1)] if kv_heads > 1 else []) + [(b, 2) for b in range(1, micro)]
 
-    def grad_copy(item, head, count):
+    def grad_copy(item, head):
         return pltpu.make_async_remote_copy(
-            src_ref=g_out.at[item, pl.ds(head, count)],
-            dst_ref=g_in.at[item, pl.ds(head, count)],
+            src_ref=g_out.at[item, head],
+            dst_ref=g_in.at[item, head],
             send_sem=g_send,
             recv_sem=g_recv.at[item, head],
             device_id=(section - 1, block),
@@ -141,7 +141,7 @@
             src_ref=part_send.at[item],
             dst_ref=part_recv.at[item],
             send_sem=part_send_sem,
-            recv_sem=part_recv_sem,
+            recv_sem=part_recv_sem.at[item],
             device_id=(section, block - 1),
             device_id_type=MESH,
         )
@@ -301,7 +301,8 @@
         b, _, wide_col = place(item)
         for head, count in messages:
             if grad_of is sent_grad:
-                grad_copy(item, head, count).wait_recv()
+                for i in range(count):
+                    grad_copy(item, head + i).wait_recv()
             beside(head, count, True)
             cols = slice(head * DH, (head + count) * DH)
             value = rows_of(1, item)
@@ -320,7 +321,8 @@
 
             @pl.when(has_next)
             def _():
-                grad_copy(item, head, count).start()
+                for i in range(count):
+                    grad_copy(item, head + i).start()
 
             for i in range(count):
                 at = pl.multiple_of(wide_col + (head + i) * DH, DH)
@@ -368,7 +370,7 @@
         return behind
 
     def one_sent(item):
-        backward(item, inner, sent_grad, behind_of(item - 1, inner[-1][0]))
+        backward(item, edge, sent_grad, behind_of(item - 1, group // 2))
         send_part(item - 1)
 
     def last_sent():
@@ -387,14 +389,14 @@
             wait_later(b)
 
         def both(item):
-            behind = behind_of(item - 1, inner[-1][0])
+            behind = behind_of(item - 1, group // 2)
 
             def beside(head, count, first):
                 behind(head, count, first)
                 if not first:
                     probabilities(item + lead, head, count)
 
-            backward(item, inner, sent_grad, beside)
+            backward(item, edge, sent_grad, beside)
             send_part(item - 1)
 
         loop(1, items - lead, both)
@@ -413,11 +415,11 @@
         loop(1, items - 1, one_sent)
         last_sent()
 
-    @pl.when(has_right)
-    def _():
-        pltpu.make_async_copy(part_recv, part_recv, part_recv_sem).wait()
-
     def finish(item):
+        @pl.when(has_right)
+        def _():
+            part_copy(item).wait_recv()
+
         b, col, _ = place(item)
         for i in range(2):
             total = part_own[item, i] + part_recv[item, i].astype(jnp.float32)
@@ -511,7 +513,7 @@
             dma(()),
             dma((items, group)),
             dma(()),
-            dma(()),
+            dma((items,)),
             dma(()),
             dma((2,)),
         ],

time: 47.9 us -> 46.4 us (0.969)
  Pallas kernels: 47.2 us -> 45.6 us
    pallas_call x1, Pallas kernels: 44.9 us -> 43.4 us  [per_device(): pl.pallas_call(functools.partial(kernel, sections, seq_size, kv_heads, gr...]
where the time goes in v6:
time: 46.4 us; the launch traced here: 46.3 us
  Pallas kernels  45.6 us (98%)
  between operations  0.64 us (1%)
    pallas_call x1, Pallas kernels, per_device(): pl.pallas_call(functools.partial(kernel, sections, seq_size, kv_heads, gr...  43.4 us
    pallas_call x1, Pallas kernels, per_device(): pl.pallas_call(hand_over, out_shape=shapes, in_specs=[anywhere] * 3, out_...  2.28 us

profile of v6, /device:TPU:1, one launch (start us, length us, event | category | flops | bytes accessed | tf_op | source)
XLA Modules:
  0.0 46.3 jit_solution(5669938259163548949)
XLA Ops:
  0.6 43.4 %shard_map.76 = (bf16[1,2,128,2048]{3,2,1,0:T(8,128)(2,1)}, bf16[1,2,128,512]{3,2,1,0:T(8,128)(2,1)}, bf16[1,2,128,512]{3,2,1,0:T(8,128)(2,1)}) custom-call(bf16[1,2,128,2048]{3,2,1,0:T(8,128)(2,1)} %q_hbm.1, bf16[1,2,128,512]{3,2,1,0:T(8,128)(2,1)} %k_hbm.1, bf16[1,2,128,512]{3,2,1,0:T(8,128)(2,1)} %v_hbm.1, bf16[2,128,2048]{2,1,0:T(8,128)(2,1)} %g_hbm.1, ...), custom_call_target="tpu_custom_call" | custom-call | flops 1342177280 | bytes 6291456 | tf_op jit(solution)/shard_map/pallas_call | solution.py:485
  44.0 2.3 %shard_map.77 = (bf16[1,2,128,2048]{3,2,1,0:T(8,128)(2,1)}, bf16[1,2,128,512]{3,2,1,0:T(8,128)(2,1)}, bf16[1,2,128,512]{3,2,1,0:T(8,128)(2,1)}) custom-call(bf16[1,2,128,2048]{3,2,1,0:T(8,128)(2,1)} %get-tuple-element.6.refs_0_, bf16[1,2,128,512]{3,2,1,0:T(8,128)(2,1)} %get-tuple-element.7.refs_1_, bf16[1,2,128,512]{3,2,1,0:T(8,128)(2,1)} %get-tuple-element.8.refs_2_), custom_call_target="tpu_custom_call" | custom-call | tf_op jit(solution)/shard_map/pallas_call | solution.py:529

commit v7 on v6

--- a/solution.py
+++ b/solution.py
@@ -374,9 +374,18 @@
         send_part(item - 1)
 
     def last_sent():
-        backward(items - 1, edge, sent_grad, behind_of(items - 2, 1))
-        send_part(items - 2)
-        both_grads(items - 1, sent_grad)
+        behind = behind_of(items - 2, 0)
+
+        def beside(head, count, first):
+            behind(head, count, first)
+            if first and head == 1:
+                send_part(items - 2)
+            if not first and head == group - 1:
+                value_grad(items - 1, sent_grad)
+
+        backward(items - 1, edge, sent_grad, beside)
+        key_grad(items - 1)
+        send_part(items - 1)
 
     @pl.when(section == sections - 2)
     def _():

time: 46.4 us -> 45.8 us (0.987)
  Pallas kernels: 45.6 us -> 45 us
    pallas_call x1, Pallas kernels: 43.4 us -> 42.7 us  [per_device(): pl.pallas_call(functools.partial(kernel, sections, seq_size, kv_heads, gr...]
where the time goes in v7:
time: 45.8 us; the launch traced here: 45.6 us
  Pallas kernels  45 us (98%)
  between operations  0.64 us (1%)
    pallas_call x1, Pallas kernels, per_device(): pl.pallas_call(functools.partial(kernel, sections, seq_size, kv_heads, gr...  42.7 us
    pallas_call x1, Pallas kernels, per_device(): pl.pallas_call(hand_over, out_shape=shapes, in_specs=[anywhere] * 3, out_...  2.28 us

profile of v7, /device:TPU:1, one launch (start us, length us, event | category | flops | bytes accessed | tf_op | source)
XLA Modules:
  0.0 45.6 jit_solution(16026024620338983957)
XLA Ops:
  0.6 42.7 %shard_map.76 = (bf16[1,2,128,2048]{3,2,1,0:T(8,128)(2,1)}, bf16[1,2,128,512]{3,2,1,0:T(8,128)(2,1)}, bf16[1,2,128,512]{3,2,1,0:T(8,128)(2,1)}) custom-call(bf16[1,2,128,2048]{3,2,1,0:T(8,128)(2,1)} %q_hbm.1, bf16[1,2,128,512]{3,2,1,0:T(8,128)(2,1)} %k_hbm.1, bf16[1,2,128,512]{3,2,1,0:T(8,128)(2,1)} %v_hbm.1, bf16[2,128,2048]{2,1,0:T(8,128)(2,1)} %g_hbm.1, ...), custom_call_target="tpu_custom_call" | custom-call | flops 1342177280 | bytes 6291456 | tf_op jit(solution)/shard_map/pallas_call | solution.py:494
  43.3 2.3 %shard_map.77 = (bf16[1,2,128,2048]{3,2,1,0:T(8,128)(2,1)}, bf16[1,2,128,512]{3,2,1,0:T(8,128)(2,1)}, bf16[1,2,128,512]{3,2,1,0:T(8,128)(2,1)}) custom-call(bf16[1,2,128,2048]{3,2,1,0:T(8,128)(2,1)} %get-tuple-element.6.refs_0_, bf16[1,2,128,512]{3,2,1,0:T(8,128)(2,1)} %get-tuple-element.7.refs_1_, bf16[1,2,128,512]{3,2,1,0:T(8,128)(2,1)} %get-tuple-element.8.refs_2_), custom_call_target="tpu_custom_call" | custom-call | tf_op jit(solution)/shard_map/pallas_call | solution.py:538
